TPU v7x, 32 devices: a whole 2x2x4 slice. The times are simulated.
32 devices in a mesh: dp: 4 (over y, core), expert: 8 (over z, x).
Axes of the slice: x: 2, y: 2, z: 4, core: 2. Of those that a mesh axis runs over, the one named last changes fastest.
Arguments:
- tokens: bfloat16 [2048, 2048], P(('dp', 'expert')), may hold values from -6 to 6
- expert_ids: int32 [2048, 8], P(('dp', 'expert')), may hold values from 0 to 127, all different within a row; in each aligned block of 64 rows (0 to 63, 64 to 127, ...) at most 8 rows name the same one
- gate_weight: bfloat16 [8, 2048, 768], P('expert', 'dp'), may hold values from -0.125 to 0.125
- up_weight: bfloat16 [8, 2048, 768], P('expert', 'dp'), may hold values from -0.125 to 0.125
- down_weight: bfloat16 [8, 768, 2048], P('expert', None, 'dp'), may hold values from -6 to 6
Outputs:
- factor: float32 [8, 768, 768], P('expert', 'dp')
- whitened: float32 [8, 768, 2048], P('expert', None, 'dp')
Inputs may be any that keep to these rules, and one draw needn't show every extreme that they name: `expert_ids`: each row names 8 different experts. Among the rows of one device (aligned blocks of 64 rows) no expert is named more than 8 times, a bound that some block reaches. Only experts below 8 enter the outputs.
All inputs are finite; a program needn't handle non-finite values.
Results may differ from a plain program's by a relative error of at most 0.0035.
Values may be sent and summed in bfloat16 or wider, within the bound.
No kernel may reach another device: no remote copies, remote signals or barrier semaphores. Data moves between devices by JAX's collectives and lax.ppermute only.
A program may use at most 128 MiB of HBM per device.

v0:
```python
import jax
import jax.numpy as jnp
from jax import lax
from jax.sharding import PartitionSpec as P

CAP = 8


damping = 0.02
highest = lax.Precision.HIGHEST


def upper_factor(gram_sum):
    return jnp.linalg.cholesky(gram_sum).T


def body(tokens, expert_ids, gate_weight, up_weight, down_weight):
    owners = lax.axis_size("expert") * gate_weight.shape[0]
    tok_rows = tokens.shape[0]
    capacity = CAP
    expert_range = jnp.arange(owners, dtype=jnp.int32)
    member = jnp.any(expert_ids[:, :, None] == expert_range[None, None, :], axis=1)
    earlier = (jnp.arange(tok_rows)[:, None] > jnp.arange(tok_rows)[None, :]).astype(jnp.int32)
    ranking = jnp.dot(earlier, member.astype(jnp.int32))
    slot_range = jnp.arange(capacity, dtype=jnp.int32)
    placing = (member[:, :, None] & (ranking[:, :, None] == slot_range[None, None, :])).astype(
        jnp.bfloat16
    )
    outgoing = jnp.einsum(
        "tec,td->ecd", placing, tokens, preferred_element_type=jnp.float32
    ).astype(jnp.bfloat16)
    arrived = lax.all_to_all(outgoing, "expert", split_axis=0, concat_axis=0, tiled=True)
    received_rows = arrived.reshape(-1, arrived.shape[-1])
    slot_total = received_rows.shape[0]
    gate_sum = jnp.dot(
        received_rows,
        lax.all_gather(gate_weight, "dp", axis=1, tiled=True)[0],
        preferred_element_type=jnp.float32,
    )
    up_sum = jnp.dot(
        received_rows,
        lax.all_gather(up_weight, "dp", axis=1, tiled=True)[0],
        preferred_element_type=jnp.float32,
    )
    gate_sum, up_sum = (gate_sum, up_sum)
    hidden = (jax.nn.silu(gate_sum) * up_sum).astype(jnp.bfloat16)
    hidden_width = hidden.shape[1]
    identity = jnp.eye(hidden_width, dtype=jnp.float32)
    local_gram = (
        jnp.einsum("rf,rg->fg", hidden, hidden, preferred_element_type=jnp.float32) / slot_total
    )
    running_gram = lax.psum(local_gram, "dp") + damping * identity
    factor = upper_factor(running_gram)
    row_share = hidden_width // lax.axis_size("dp")
    own_rows = lax.dynamic_slice_in_dim(factor, lax.axis_index("dp") * row_share, row_share, 0)
    whitened = jnp.dot(factor, down_weight[0].astype(jnp.float32), precision=highest)
    return (own_rows[None], whitened[None])


def solution(mesh):
    return jax.shard_map(
        body,
        mesh=mesh,
        in_specs=(
            P(("dp", "expert"), None),
            P(("dp", "expert"), None),
            P("expert", "dp", None),
            P("expert", "dp", None),
            P("expert", None, "dp"),
        ),
        out_specs=(P("expert", "dp", None), P("expert", None, "dp")),
        check_vma=False,
    )
```

profile of v0, /device:TPU:0, one launch (start us, length us, event | category | flops | bytes accessed | tf_op | source)
XLA Modules:
  0.0 301.3 jit_solution(11818738526485425487)
XLA Ops:
  9.5 1.2 convolution_convert_fusion
  10.7 16.0 %all_to_all.5 = bf16[8,8,2048]{2,1,0:T(8,128)(2,1)S(1)} all-to-all(bf16[8,8,2048]{2,1,0:T(8,128)(2,1)S(1)} %convolution_convert_fusion), channel_id=1, replica_groups=mesh['dp'=4,'expert'=8] {'expert'}, dimensions={0} | all-to-all | bytes 524288 | tf_op jit(solution)/shard_map/all_to_all | solution.py:32
  26.7 14.2 %all-gather.3.cloned.1.call-done = bf16[1,2048,768]{2,1,0:T(8,128)(2,1)} async-done(((bf16[1,512,768]{2,1,0:T(8,128)(2,1)}), bf16[1,2048,768]{2,1,0:T(8,128)(2,1)}) %all-gather.3.cloned.1.call-update) | async-done | bytes 3145744 | tf_op jit(solution)/shard_map/all_gather | solution.py:37
  40.8 2.5 fusion.2
  43.4 27.6 %all-gather.5.cloned.1.call-done = bf16[1,2048,768]{2,1,0:T(8,128)(2,1)} async-done(((bf16[1,512,768]{2,1,0:T(8,128)(2,1)}), bf16[1,2048,768]{2,1,0:T(8,128)(2,1)}) %all-gather.5.cloned.1.call-update) | async-done | bytes 3145744 | tf_op jit(solution)/shard_map/all_gather | solution.py:42
  71.0 5.9 %convolution_multiply_fusion = f32[768,768]{0,1:T(8,128)} fusion(bf16[1,2048,768]{2,1,0:T(8,128)(2,1)} %all-gather.5.cloned.1.call-done, bf16[8,8,2048]{2,1,0:T(8,128)(2,1)S(1)} %all_to_all.5, f32[64,768]{1,0:T(8,128)S(1)} %fusion.2), kind=kOutput, calls=%fused_computation.11 | convolution fusion | flops 277708800 | bytes 5963776 | tf_op jit(solution)/shard_map/rf,rg->fg/dot_general | solution.py:50
  76.9 55.8 %all-reduce.3.cloned.1.call-done = f32[768,768]{0,1:T(8,128)} async-done(((f32[768,768]{0,1:T(8,128)}), f32[768,768]{0,1:T(8,128)}) %all-reduce.3.cloned.1.call-update) | async-done | bytes 2359312 | tf_op jit(solution)/shard_map/psum | solution.py:52
  132.7 3.3 %select_add_fusion = f32[768,768]{0,1:T(8,128)} fusion(f32[768,768]{0,1:T(8,128)} %all-reduce.3.cloned.1.call-done), kind=kLoop, calls=%fused_computation.7 | loop fusion | flops 1769472 | bytes 4718592 | tf_op jit(solution)/shard_map/add | solution.py:52
  136.0 3.3 %copy.17 = f32[768,768]{1,0:T(8,128)} copy(f32[768,768]{0,1:T(8,128)} %select_add_fusion) | data formatting | bytes 4718592 | tf_op jit(solution)/shard_map/add | solution.py:52
  139.3 2.0 fusion.4
  141.3 1.4 copy-done.2
  142.7 11.7 %cholesky.164 = f32[128,128]{1,0:T(8,128)S(1)} custom-call(f32[128,128]{1,0:T(8,128)S(1)} %cholesky.421), custom_call_target="Cholesky" | custom-call | tf_op jit(solution)/shard_map/jit(cholesky)/cholesky | solution.py:14
  154.6 9.8 %custom-call.43 = f32[1,128,128]{1,2,0:T(8,128)S(1)} custom-call(f32[1,128,128]{2,1,0:T(8,128)S(1)} %get-tuple-element.11), custom_call_target="InvertDiagBlocksLowerTriangular" | custom-call | tf_op jit(solution)/shard_map/jit(cholesky)/cholesky | solution.py:14
  164.5 1.5 constant_dynamic-update-slice_fusion.4
  166.0 1.7 convolution_subtract_fusion
  168.3 12.5 %cholesky.187 = f32[128,128]{1,0:T(8,128)S(1)} custom-call(f32[128,128]{1,0:T(8,128)} %cholesky.425), custom_call_target="Cholesky" | custom-call | tf_op jit(solution)/shard_map/jit(cholesky)/cholesky | solution.py:14
  182.1 0.9 copy.19
  183.1 11.5 %custom-call.44 = f32[1,128,128]{1,2,0:T(8,128)} custom-call(f32[1,128,128]{2,1,0:T(8,128)} %get-tuple-element.9), custom_call_target="InvertDiagBlocksLowerTriangular" | custom-call | tf_op jit(solution)/shard_map/jit(cholesky)/cholesky | solution.py:14
  194.5 1.3 convolution_dynamic-update-slice_fusion
  195.8 1.9 convolution_subtract_fusion.1
  197.8 11.7 %cholesky.352 = f32[128,128]{1,0:T(8,128)S(1)} custom-call(f32[128,128]{1,0:T(8,128)S(1)} %cholesky.430), custom_call_target="Cholesky" | custom-call | tf_op jit(solution)/shard_map/jit(cholesky)/cholesky | solution.py:14
  210.2 10.6 %custom-call.45 = f32[1,128,128]{1,2,0:T(8,128)S(1)} custom-call(f32[1,128,128]{2,1,0:T(8,128)} %get-tuple-element.7), custom_call_target="InvertDiagBlocksLowerTriangular" | custom-call | tf_op jit(solution)/shard_map/jit(cholesky)/cholesky | solution.py:14
  221.3 2.1 convolution_subtract_fusion.2
  223.4 12.1 %cholesky.371 = f32[128,128]{1,0:T(8,128)S(1)} custom-call(f32[128,128]{1,0:T(8,128)S(1)} %cholesky.435), custom_call_target="Cholesky" | custom-call | tf_op jit(solution)/shard_map/jit(cholesky)/cholesky | solution.py:14
  235.6 9.8 %custom-call.46 = f32[1,128,128]{1,2,0:T(8,128)S(1)} custom-call(f32[1,128,128]{2,1,0:T(8,128)S(1)} %get-tuple-element.5), custom_call_target="InvertDiagBlocksLowerTriangular" | custom-call | tf_op jit(solution)/shard_map/jit(cholesky)/cholesky | solution.py:14
  245.8 1.9 convolution_subtract_fusion.3
  247.7 11.7 %cholesky.390 = f32[128,128]{1,0:T(8,128)S(1)} custom-call(f32[128,128]{1,0:T(8,128)S(1)} %cholesky.440), custom_call_target="Cholesky" | custom-call | tf_op jit(solution)/shard_map/jit(cholesky)/cholesky | solution.py:14
  259.6 9.8 %custom-call.47 = f32[1,128,128]{1,2,0:T(8,128)S(1)} custom-call(f32[1,128,128]{2,1,0:T(8,128)S(1)} %get-tuple-element.3), custom_call_target="InvertDiagBlocksLowerTriangular" | custom-call | tf_op jit(solution)/shard_map/jit(cholesky)/cholesky | solution.py:14
  269.7 1.7 convolution_subtract_fusion.4
  271.4 11.7 %cholesky.408 = f32[128,128]{1,0:T(8,128)S(1)} custom-call(f32[128,128]{1,0:T(8,128)S(1)} %convolution_subtract_fusion.4), custom_call_target="Cholesky" | custom-call | tf_op jit(solution)/shard_map/jit(cholesky)/cholesky | solution.py:14
  290.6 3.2 %convolution_bitcast_fusion = f32[1,768,512]{2,1,0:T(8,128)} fusion(f32[768,768]{0,1:T(8,128)S(1)} %select_select_fusion, bf16[1,768,512]{2,1,0:T(8,128)(2,1)S(1)} %copy-done), kind=kOutput, calls=%fused_computation.12 | convolution fusion | flops 3623878656 | bytes 4718592 | tf_op jit(solution)/shard_map/dot_general | solution.py:56
  293.7 0.9 dynamic-slice_bitcast_fusion
  (46 shorter events, 10.2 us)
Async XLA Ops:
  7.2 283.4 %copy-start = (bf16[1,768,512]{2,1,0:T(8,128)(2,1)S(1)}, bf16[1,768,512]{2,1,0:T(8,128)(2,1)}, u32[]{:S(2)}) copy-start(bf16[1,768,512]{2,1,0:T(8,128)(2,1)} %param.9) | copy-start | bytes 2359300
  7.2 33.7 %all-gather.3.cloned.1.call-start = ((), (), s32[]{:S(2)}) async-start(), calls=%async_computation.1 | async-start | bytes 3932160 | tf_op jit(solution)/shard_map/all_gather | solution.py:37
  7.9 63.1 %all-gather.5.cloned.1.call-start = ((), (), s32[]{:S(2)}) async-start(), calls=%async_computation.2 | async-start | bytes 3932160 | tf_op jit(solution)/shard_map/all_gather | solution.py:42
  8.7 124.0 %all-reduce.3.cloned.1.call-start = ((), (), s32[]{:S(2)}) async-start(), calls=%async_computation.3 | async-start | bytes 4718592 | tf_op jit(solution)/shard_map/psum | solution.py:52
  136.0 3.3 %copy-start.1 = (f32[768,768]{0,1:T(8,128)S(1)}, f32[768,768]{0,1:T(8,128)}, u32[]{:S(2)}) copy-start(f32[768,768]{0,1:T(8,128)} %all-reduce.3.cloned.1.call-done) | copy-start | bytes 7077892
  141.3 1.4 copy-start.2
  180.9 0.6 copy-start.3
Sparse Core Ops, SparseCore 0:
  9.6 31.2 all-gather.2
  42.4 28.5 all-gather.4
  77.0 55.6 all-reduce.2
where the time goes:
time: 305 us; the launch traced here: 301 us
  other arithmetic  134 us (44%)
  waiting for transfers between devices  98.9 us (32%)
  matrix products  25.9 us (8%)
  between operations  18 us (6%)
  blocking collectives  16 us (5%)
  local copies, waits for them, and re-layouts  8.45 us (3%)
    another operation x22, other arithmetic, upper_factor(): return jnp.linalg.cholesky(gram_sum).T  128 us
    psum x1, waiting for transfers between devices, body(): running_gram = lax.psum(local_gram, 'dp') + damping * identity  55.8 us
    all_gather x1, waiting for transfers between devices, body(): lax.all_gather(up_weight, 'dp', axis=1, tiled=True)[0]  27.6 us
    all_to_all x1, blocking collectives, body(): lax.all_to_all(outgoing, 'expert', split_axis=0, concat_axis=0, tiled=True)  16 us
    all_gather x1, waiting for transfers between devices, body(): lax.all_gather(gate_weight, 'dp', axis=1, tiled=True)[0]  14.2 us
    another operation x10, matrix products, upper_factor(): return jnp.linalg.cholesky(gram_sum).T  13 us
  transfers between devices with their start and end apart: 3, of which 3 were waited for; matrix products, arithmetic and copies ran while one was open for 1% of the time, Pallas kernels for 0%

commit v1 on v0

v1 whole, which is shorter than its diff:
```python
import functools

import jax
import jax.numpy as jnp
from jax import lax
from jax.experimental import pallas as pl
from jax.experimental.pallas import tpu as pltpu
from jax.sharding import PartitionSpec as P

CAP = 8
CORES = 2
PANEL = 128
WINDOW = 16
damping = 0.02
highest = lax.Precision.HIGHEST
f32 = jnp.float32
bf16 = jnp.bfloat16


def reciprocal(value):
    guess = pl.reciprocal(value, approx=True)
    return guess * (2.0 - value * guess)


def factor_block(a_ref, u_ref, inverse_ref, start):
    row_in_window = lax.broadcasted_iota(jnp.int32, (WINDOW, PANEL), 0)
    lane = lax.broadcasted_iota(jnp.int32, (WINDOW, PANEL), 1)
    lane8 = lax.broadcasted_iota(jnp.int32, (8, PANEL), 1)
    row8 = lax.broadcasted_iota(jnp.int32, (8, PANEL), 0)
    groups = PANEL // 8
    per_window = WINDOW // 8
    left = [a_ref[start + 8 * i : start + 8 * i + 8, start : start + PANEL] for i in range(groups)]
    right = [(lane8 == row8 + 8 * i).astype(f32) for i in range(groups)]
    for window in range(PANEL // WINDOW):
        k = window * WINDOW
        first = window * per_window
        rows_l = jnp.concatenate(left[first : first + per_window], 0)
        rows_r = jnp.concatenate(right[first : first + per_window], 0)
        columns = [
            jnp.broadcast_to(rows_l[:, k + c : k + c + 1], (WINDOW, PANEL)) for c in range(WINDOW)
        ]
        upper_l = jnp.zeros((WINDOW, PANEL), f32)
        upper_r = jnp.zeros((WINDOW, PANEL), f32)
        pivots = jnp.zeros((WINDOW, PANEL), f32)
        for r in range(WINDOW):
            here = row_in_window == r
            pivot = columns[r][r : r + 1, :]
            ratio = jnp.where(here, 0.0, columns[r]) * reciprocal(pivot)
            pivot_l, pivot_r = rows_l[r : r + 1, :], rows_r[r : r + 1, :]
            upper_l = jnp.where(here, pivot_l, upper_l)
            upper_r = jnp.where(here, pivot_r, upper_r)
            pivots = jnp.where(here, pivot, pivots)
            rows_l = rows_l - ratio * pivot_l
            rows_r = rows_r - ratio * pivot_r
            for c in range(r + 1, WINDOW):
                columns[c] = columns[c] - ratio * columns[c][r : r + 1, :]
        inverse, root = reciprocal(pivots), lax.rsqrt(pivots)
        rows_l, rows_r = rows_l * inverse, rows_r * inverse
        u_ref[start + k : start + k + WINDOW, start : start + PANEL] = jnp.where(
            lane >= row_in_window + k, upper_l * root, 0.0
        )
        inverse_ref[k : k + WINDOW, :] = upper_r * root
        for i in range(first + per_window, groups):
            old, new_l, new_r = left[i], left[i], right[i]
            for c in range(WINDOW):
                scale = jnp.broadcast_to(old[:, k + c : k + c + 1], (8, PANEL))
                new_l = new_l - scale * rows_l[c : c + 1, :]
                new_r = new_r - scale * rows_r[c : c + 1, :]
            left[i], right[i] = new_l, new_r


def transposed_dot(a, b, precision=None):
    return lax.dot_general(
        a, b, (((0,), (0,)), ((), ())), preferred_element_type=f32, precision=precision
    )


def whiten_kernel(scale, index_ref, hidden_ref, down_ref, factor_ref, out_ref, a_ref, u_ref, inverse_ref):
    width = hidden_ref.shape[1]
    blocks = width // PANEL
    u_ref[...] = jnp.zeros_like(u_ref)
    for b in range(blocks):
        s = b * PANEL
        gram = transposed_dot(hidden_ref[:, s : s + PANEL], hidden_ref[:, s:]) * scale
        row = lax.broadcasted_iota(jnp.int32, gram.shape, 0)
        lane = lax.broadcasted_iota(jnp.int32, gram.shape, 1)
        a_ref[s : s + PANEL, s:] = jnp.where(row == lane, gram + damping, gram)
    for p in range(blocks):
        s, e = p * PANEL, (p + 1) * PANEL
        factor_block(a_ref, u_ref, inverse_ref, s)
        if e < width:
            panel = jnp.dot(
                inverse_ref[...], a_ref[s:e, e:], preferred_element_type=f32, precision=highest
            )
            u_ref[s:e, e:] = panel
            for b in range(p + 1, blocks):
                t = b * PANEL
                a_ref[t : t + PANEL, t:] = a_ref[t : t + PANEL, t:] - transposed_dot(
                    panel[:, t - e : t - e + PANEL], panel[:, t - e :], highest
                )
        rows = u_ref[s:e, s:]
        high = rows.astype(bf16)
        low = (rows - high.astype(f32)).astype(bf16)
        down = down_ref[s:, :]
        out_ref[s:e, :] = jnp.dot(high, down, preferred_element_type=f32) + jnp.dot(
            low, down, preferred_element_type=f32
        )
    share = factor_ref.shape[0]
    factor_ref[...] = u_ref[pl.ds(pl.multiple_of(index_ref[0] * share, 8), share), :]


def whiten(index, hidden, down, share, slot_total):
    width, columns = down.shape
    vmem = pl.BlockSpec(memory_space=pltpu.VMEM)
    return pl.pallas_call(
        functools.partial(whiten_kernel, 1.0 / slot_total),
        out_shape=(
            jax.ShapeDtypeStruct((share, width), f32),
            jax.ShapeDtypeStruct((width, columns), f32),
        ),
        in_specs=[pl.BlockSpec(memory_space=pltpu.SMEM), vmem, vmem],
        out_specs=(vmem, vmem),
        scratch_shapes=[
            pltpu.VMEM((width, width), f32),
            pltpu.VMEM((width, width), f32),
            pltpu.VMEM((PANEL, PANEL), f32),
        ],
        compiler_params=pltpu.CompilerParams(vmem_limit_bytes=48 * 2**20),
        name="whiten",
    )(index, hidden, down)


def hidden_kernel(index_ref, token_ref, weight_ref, out_ref):
    chunks, depth, both = weight_ref.shape
    width = both // 2
    total = None
    for j in range(chunks):
        at = pl.multiple_of(index_ref[j] * depth, depth)
        part = jnp.dot(token_ref[:, pl.ds(at, depth)], weight_ref[j], preferred_element_type=f32)
        total = part if total is None else total + part
    gate, up = total[:, :width], total[:, width:]
    hidden = (gate / (1.0 + jnp.exp(-gate)) * up).astype(bf16)
    sources = chunks // CORES
    rows = hidden.shape[0] // sources
    for k in range(sources):
        at = pl.multiple_of(index_ref[chunks + k] * rows, 16)
        out_ref[pl.ds(at, rows), :] = hidden[k * rows : (k + 1) * rows]


def project(chunk_index, tokens, weights):
    vmem = pl.BlockSpec(memory_space=pltpu.VMEM)
    return pl.pallas_call(
        hidden_kernel,
        out_shape=jax.ShapeDtypeStruct((tokens.shape[0], weights.shape[2] // 2), bf16),
        in_specs=[pl.BlockSpec(memory_space=pltpu.SMEM), vmem, vmem],
        out_specs=vmem,
        compiler_params=pltpu.CompilerParams(vmem_limit_bytes=48 * 2**20),
        name="project",
    )(chunk_index, tokens, weights)


def body(tokens, expert_ids, gate_weight, up_weight, down_weight):
    experts = lax.axis_size("expert")
    owners = experts * gate_weight.shape[0]
    dp_size = lax.axis_size("dp")
    chips = dp_size // CORES
    dp = lax.axis_index("dp")
    chip, core = dp // CORES, dp % CORES
    width = gate_weight.shape[2]
    share = width // chips

    def to_chip(x, k):
        steps = [(i, (i + k * CORES) % dp_size) for i in range(dp_size)]
        return lax.ppermute(x, "dp", steps)

    def to_core(x):
        return lax.ppermute(x, "dp", [(i, i ^ 1) for i in range(dp_size)])

    def weight_block(owner):
        at = owner * share
        return jnp.concatenate(
            [
                lax.dynamic_slice_in_dim(gate_weight[0], at, share, 1),
                lax.dynamic_slice_in_dim(up_weight[0], at, share, 1),
            ],
            1,
        )

    blocks = [weight_block(chip)]
    for k in range(1, chips):
        blocks.append(to_chip(weight_block((chip + k) % chips), k))
    sources = [(chip - k + chips) % chips for k in range(chips)]
    blocks = blocks + [to_core(block) for block in blocks]
    chunk_index = jnp.stack(
        [source * CORES + core for source in sources]
        + [source * CORES + 1 - core for source in sources]
        + sources
    ).astype(jnp.int32)

    tok_rows = tokens.shape[0]
    expert_range = jnp.arange(owners, dtype=jnp.int32)
    member = jnp.any(expert_ids[:, :, None] == expert_range[None, None, :], axis=1)
    earlier = (jnp.arange(tok_rows)[:, None] > jnp.arange(tok_rows)[None, :]).astype(jnp.int32)
    ranking = jnp.dot(earlier, member.astype(jnp.int32))
    slot_range = jnp.arange(CAP, dtype=jnp.int32)
    placing = (member[:, :, None] & (ranking[:, :, None] == slot_range[None, None, :])).astype(bf16)
    outgoing = jnp.einsum("tec,td->ecd", placing, tokens, preferred_element_type=f32).astype(bf16)
    arrived = lax.all_to_all(outgoing, "expert", split_axis=0, concat_axis=0, tiled=True)
    received = arrived.reshape(-1, arrived.shape[-1])
    slot_total = received.shape[0]

    slots = jnp.concatenate([received] + [to_chip(received, k) for k in range(1, chips)], 0)
    hidden = project(chunk_index, slots, jnp.stack(blocks))

    pieces = jnp.stack([hidden] + [to_chip(hidden, k) for k in range(1, chips)])
    ordered = jnp.roll(pieces[::-1], chip + 1, axis=0)
    whole = jnp.moveaxis(ordered, 0, 1).reshape(chips * slot_total, width)
    whole = jnp.concatenate([whole, to_core(whole)], 0)
    factor, whitened = whiten(
        dp.astype(jnp.int32)[None], whole, down_weight[0], width // dp_size, slot_total
    )
    return (factor[None], whitened[None])


def solution(mesh):
    return jax.shard_map(
        body,
        mesh=mesh,
        in_specs=(
            P(("dp", "expert"), None),
            P(("dp", "expert"), None),
            P("expert", "dp", None),
            P("expert", "dp", None),
            P("expert", None, "dp"),
        ),
        out_specs=(P("expert", "dp", None), P("expert", None, "dp")),
        check_vma=False,
    )
```

time: 305 us -> 71.3 us (0.23); the launches traced: 301 us -> 71 us
  other arithmetic: 134 us -> 3.74 us
  waiting for transfers between devices: 98.9 us -> 21 us
  Pallas kernels: 0 us -> 30.3 us
  matrix products: 25.9 us -> 1.06 us
  between operations: 18 us -> 0.79 us
  blocking collectives: 16 us -> 0 us
  starting transfers between devices: 0.11 us -> 12.4 us
  local copies, waits for them, and re-layouts: 8.45 us -> 1.66 us
    another operation x22 -> x3, other arithmetic: 128 us -> 2.62 us  [the longest x2 2.59 us: body(): hidden = project(chunk_index, slots, jnp.stack(blocks))]
    psum x1 -> x0, waiting for transfers between devices: 55.8 us -> none  [body(): running_gram = lax.psum(local_gram, 'dp') + damping * identity]
    all_gather x2 -> x0, waiting for transfers between devices: 41.8 us -> none  [the longest x1 27.6 us: body(): lax.all_gather(up_weight, 'dp', axis=1, tiled=True)[0]]
    pallas_call x0 -> x2, Pallas kernels: none -> 30.3 us  [the longest x1 29.2 us: whiten(): pl.pallas_call(functools.partial(whiten_kernel, 1.0 / slot_total), out_sh...]
    ppermute x0 -> x6, waiting for transfers between devices: none -> 21 us  [the longest x3 19.6 us: to_chip(): return lax.ppermute(x, 'dp', steps)]
    all_to_all x1 -> x0, blocking collectives: 16 us -> none  [body(): lax.all_to_all(outgoing, 'expert', split_axis=0, concat_axis=0, tiled=True)]
    another operation x10 -> x0, matrix products: 13 us -> none  [upper_factor(): return jnp.linalg.cholesky(gram_sum).T]
    dot_general x4 -> x1, matrix products: 12.8 us -> 0.93 us  [body(): jnp.einsum('tec,td->ecd', placing, tokens, preferred_element_type=f32)]
  transfers between devices with their start and end apart: 3 -> 7, of which waited for: 3 -> 4; matrix products, arithmetic and copies ran while one was open for 1% -> 3% of each run, Pallas kernels for 0% -> 0%
where the time goes in v1:
time: 71.3 us; the launch traced here: 71 us
  Pallas kernels  30.3 us (42%)
  waiting for transfers between devices  21 us (29%)
  starting transfers between devices  12.4 us (17%)
  other arithmetic  3.74 us (5%)
  local copies, waits for them, and re-layouts  1.66 us (2%)
  matrix products  1.06 us (1%)
  between operations  0.79 us (1%)
    pallas_call x1, Pallas kernels, whiten(): pl.pallas_call(functools.partial(whiten_kernel, 1.0 / slot_total), out_sh...  29.2 us
    ppermute x3, waiting for transfers between devices, to_chip(): return lax.ppermute(x, 'dp', steps)  19.6 us
    ppermute x3, starting transfers between devices, to_chip(): return lax.ppermute(x, 'dp', steps)  6.52 us
    all_to_all x1, starting transfers between devices, body(): lax.all_to_all(outgoing, 'expert', split_axis=0, concat_axis=0, tiled=True)  5.81 us
    another operation x2, other arithmetic, body(): hidden = project(chunk_index, slots, jnp.stack(blocks))  2.59 us
    dynamic_slice x1, local copies, waits for them, and re-layouts, weight_block(): lax.dynamic_slice_in_dim(up_weight[0], at, share, 1)  1.52 us
    ppermute x3, waiting for transfers between devices, to_core(): return lax.ppermute(x, 'dp', [(i, i ^ 1) for i in range(dp_size)])  1.43 us
  transfers between devices with their start and end apart: 7, of which 4 were waited for; matrix products, arithmetic and copies ran while one was open for 3% of the time, Pallas kernels for 0%

profile of v1, /device:TPU:0, one launch (start us, length us, event | category | flops | bytes accessed | tf_op | source)
XLA Modules:
  0.0 71.0 jit_solution(3442458764972433863)
XLA Ops:
  0.6 0.0 copy-start
  0.6 0.0 copy-start.2
  0.7 1.5 %dynamic-slice_bitcast_fusion.2 = (bf16[512,384]{1,0:T(8,128)(2,1)S(1)}, bf16[512,384]{1,0:T(8,128)(2,1)S(1)}, bf16[512,384]{1,0:T(8,128)(2,1)S(1)}, bf16[512,384]{1,0:T(8,128)(2,1)S(1)}) fusion(bf16[1,512,768]{2,1,0:T(8,128)(2,1)} %param.8, s32[]{:T(128)S(6)} %select_n.43, s32[]{:T(128)S(6)} %select_n.44, bf16[1,512,768]{2,1,0:T(8,128)(2,1)} %param.7), kind=kLoop, calls=%fused_computation.10 | loop fusion | bytes 3145736 | tf_op jit(solution)/shard_map/dynamic_slice | solution.py:184
  2.2 0.9 %pad_maximum_fusion.2 = bf16[512,768]{1,0:T(8,128)(2,1)} fusion(bf16[512,384]{1,0:T(8,128)(2,1)S(1)} %get-tuple-element.11, bf16[512,384]{1,0:T(8,128)(2,1)S(1)} %get-tuple-element.12), kind=kLoop, calls=%fused_computation.3 | loop fusion | flops 1572864 | bytes 1572864 | tf_op jit(solution)/shard_map/concatenate | solution.py:181
  3.2 3.0 %collective-permute-start.1 = (bf16[512,768]{1,0:T(8,128)(2,1)}, bf16[512,768]{1,0:T(8,128)(2,1)S(1)}, u32[]{:S(2)}, u32[]{:S(2)}) collective-permute-start(bf16[512,768]{1,0:T(8,128)(2,1)} %pad_maximum_fusion.2), channel_id=1, source_target_pairs={{0,16},{8,24},{16,0},{24,8},{1,17},{9,25},{17,1},{25,9},{2,18},{10... | collective-permute-start | bytes 2359304 | tf_op jit(solution)/shard_map/ppermute | solution.py:174
  6.1 0.0 copy-done.2
  6.1 0.1 fusion.4
  6.3 0.0 copy-done
  6.3 0.9 %convolution_convert_fusion = bf16[8,8,2048]{2,1,0:T(8,128)(2,1)} fusion(bf16[64,2048]{1,0:T(8,128)(2,1)S(1)} %copy-done, s32[64,8]{0,1:T(8,128)S(1)} %fusion.4, pred[64,8]{0,1:T(8,128)(4,1)S(1)} %fusion.3), kind=kOutput, calls=%fused_computation.1 | convolution fusion | flops 16916480 | bytes 526848 | tf_op jit(solution)/shard_map/tec,td->ecd/dot_general | solution.py:207
  7.2 5.8 %all-to-all-start = ((bf16[8,8,2048]{2,1,0:T(8,128)(2,1)}), bf16[8,8,2048]{2,1,0:T(8,128)(2,1)S(1)}, u32[]{:S(2)}, u32[]{:S(2)}) async-start(bf16[8,8,2048]{2,1,0:T(8,128)(2,1)} %convolution_convert_fusion), calls=%async_computation | async-start | bytes 524288 | tf_op jit(solution)/shard_map/all_to_all | solution.py:208
  13.0 1.0 %fusion.9 = (bf16[1,512,768]{2,1,0:T(8,128)(2,1)S(1)}, bf16[512,768]{1,0:T(8,128)(2,1)}) fusion(bf16[512,384]{1,0:T(8,128)(2,1)S(1)} %get-tuple-element.10, bf16[512,384]{1,0:T(8,128)(2,1)S(1)} %get-tuple-element.13), kind=kLoop, calls=%fused_computation.24 | loop fusion | flops 1572864 | bytes 2359296 | tf_op jit(solution)/shard_map/stack | solution.py:213
  14.0 0.0 collective-permute-start.2
  14.0 9.8 %collective-permute-done.1 = bf16[512,768]{1,0:T(8,128)(2,1)S(1)} collective-permute-done((bf16[512,768]{1,0:T(8,128)(2,1)}, bf16[512,768]{1,0:T(8,128)(2,1)S(1)}, u32[]{:S(2)}, u32[]{:S(2)}) %collective-permute-start.1) | collective-permute-done | bytes 786464 | tf_op jit(solution)/shard_map/ppermute | solution.py:174
  23.9 0.0 collective-permute-start.3
  23.9 0.0 all-to-all-done
  23.9 1.7 %collective-permute-start = (bf16[64,2048]{1,0:T(8,128)(2,1)S(1)}, bf16[64,2048]{1,0:T(8,128)(2,1)S(1)}, u32[]{:S(2)}, u32[]{:S(2)}) collective-permute-start(bf16[64,2048]{1,0:T(8,128)(2,1)S(1)} %bitcast.36), channel_id=1, source_target_pairs={{0,16},{8,24},{16,0},{24,8},{1,17},{9,25},{17,1},{25,9},{2,18},{10... | collective-permute-start | bytes 786440 | tf_op jit(solution)/shard_map/ppermute | solution.py:174
  25.6 0.1 stack.51.index_ref
  25.7 6.9 %collective-permute-done = bf16[64,2048]{1,0:T(8,128)(2,1)S(1)} collective-permute-done((bf16[64,2048]{1,0:T(8,128)(2,1)S(1)}, bf16[64,2048]{1,0:T(8,128)(2,1)S(1)}, u32[]{:S(2)}, u32[]{:S(2)}) %collective-permute-start) | collective-permute-done | bytes 262176 | tf_op jit(solution)/shard_map/ppermute | solution.py:174
  32.6 0.0 collective-permute-done.2
  32.7 0.0 collective-permute-done.3
  32.7 1.6 %pad_maximum_fusion.weight_ref = bf16[4,512,768]{2,1,0:T(8,128)(2,1)S(1)} fusion(bf16[1,512,768]{2,1,0:T(8,128)(2,1)} %bitcast.16, bf16[1,512,768]{2,1,0:T(8,128)(2,1)} %bitcast.15, bf16[1,512,768]{2,1,0:T(8,128)(2,1)S(1)} %bitcast.38, bf16[1,512,768]{2,1,0:T(8,128)(2,1)S(1)} %get-tuple-element.6), kind=kLoop, calls=%fused_computation | loop fusion | flops 4718592 | bytes 6291456 | tf_op jit(solution)/shard_map/stack | solution.py:213
  34.3 0.0 copy-start.1
  34.3 1.2 %project.1 = bf16[128,384]{1,0:T(8,128)(2,1)S(1)} custom-call(s32[6]{0:T(128)S(1)} %stack.51.index_ref, bf16[128,2048]{1,0:T(8,128)(2,1)S(1)} %pad_maximum_fusion.3.token_ref, bf16[4,512,768]{2,1,0:T(8,128)(2,1)S(1)} %pad_maximum_fusion.weight_ref), custom_call_target="tpu_custom_call" | custom-call | tf_op jit(solution)/shard_map/project/pallas_call | solution.py:152
  35.4 1.8 %collective-permute-start.4 = (bf16[128,384]{1,0:T(8,128)(2,1)S(1)}, bf16[128,384]{1,0:T(8,128)(2,1)S(1)}, u32[]{:S(2)}, u32[]{:S(2)}) collective-permute-start(bf16[128,384]{1,0:T(8,128)(2,1)S(1)} %project.1), channel_id=1, source_target_pairs={{0,16},{8,24},{16,0},{24,8},{1,17},{9,25},{17,1},{25,9},{2,18},{10... | collective-permute-start | bytes 294920 | tf_op jit(solution)/shard_map/ppermute | solution.py:174
  37.2 2.9 %collective-permute-done.4 = bf16[128,384]{1,0:T(8,128)(2,1)S(1)} collective-permute-done((bf16[128,384]{1,0:T(8,128)(2,1)S(1)}, bf16[128,384]{1,0:T(8,128)(2,1)S(1)}, u32[]{:S(2)}, u32[]{:S(2)}) %collective-permute-start.4) | collective-permute-done | bytes 98336 | tf_op jit(solution)/shard_map/ppermute | solution.py:174
  40.2 0.1 fusion.2
  40.3 0.1 collective-permute-start.5
  40.4 1.4 %collective-permute-done.5 = bf16[128,768]{1,0:T(8,128)(2,1)S(1)} collective-permute-done((bf16[128,768]{1,0:T(8,128)(2,1)S(1)}, bf16[128,768]{1,0:T(8,128)(2,1)S(1)}, u32[]{:S(2)}, u32[]{:S(2)}) %collective-permute-start.5) | collective-permute-done | bytes 196640 | tf_op jit(solution)/shard_map/ppermute | solution.py:177
  41.8 0.0 copy-done.1
  41.8 29.2 %whiten.1 = (f32[192,768]{1,0:T(8,128)}, f32[768,512]{1,0:T(8,128)}) custom-call(s32[1]{0:T(128)} %bitcast.index_ref, bf16[256,768]{1,0:T(8,128)(2,1)S(1)} %pad_maximum_fusion.4.hidden_ref, bf16[768,512]{1,0:T(8,128)(2,1)S(1)} %bitcast.34), custom_call_target="tpu_custom_call" | custom-call | tf_op jit(solution)/shard_map/whiten/pallas_call | solution.py:115
  (6 shorter events, 0.1 us)
Async XLA Ops:
  0.6 5.7 %copy-start = (bf16[64,2048]{1,0:T(8,128)(2,1)S(1)}, bf16[64,2048]{1,0:T(8,128)(2,1)}, u32[]{:S(2)}) copy-start(bf16[64,2048]{1,0:T(8,128)(2,1)} %param.5) | copy-start | bytes 786436
  0.6 5.5 %copy-start.2 = (s32[64,8]{0,1:T(8,128)S(1)}, s32[64,8]{0,1:T(8,128)}, u32[]{:S(2)}) copy-start(s32[64,8]{0,1:T(8,128)} %param.6) | copy-start | bytes 6148
  3.2 20.7 %collective-permute-start.1 = (bf16[512,768]{1,0:T(8,128)(2,1)}, bf16[512,768]{1,0:T(8,128)(2,1)S(1)}, u32[]{:S(2)}, u32[]{:S(2)}) collective-permute-start(bf16[512,768]{1,0:T(8,128)(2,1)} %pad_maximum_fusion.2), channel_id=1, source_target_pairs={{0,16},{8,24},{16,0},{24,8},{1,17},{9,25},{17,1},{25,9},{2,18},{10... | collective-permute-start | bytes 2359304 | tf_op jit(solution)/shard_map/ppermute | solution.py:174
  7.2 16.7 %all-to-all-start = ((bf16[8,8,2048]{2,1,0:T(8,128)(2,1)}), bf16[8,8,2048]{2,1,0:T(8,128)(2,1)S(1)}, u32[]{:S(2)}, u32[]{:S(2)}) async-start(bf16[8,8,2048]{2,1,0:T(8,128)(2,1)} %convolution_convert_fusion), calls=%async_computation | async-start | bytes 524288 | tf_op jit(solution)/shard_map/all_to_all | solution.py:208
  14.0 18.6 %collective-permute-start.2 = (bf16[512,768]{1,0:T(8,128)(2,1)}, bf16[512,768]{1,0:T(8,128)(2,1)}, u32[]{:S(2)}, u32[]{:S(2)}) collective-permute-start(bf16[512,768]{1,0:T(8,128)(2,1)} %get-tuple-element.7), channel_id=1, source_target_pairs={{0,8},{8,0},{16,24},{24,16},{1,9},{9,1},{17,25},{25,17},{2,10},{10... | collective-permute-start | bytes 2359304 | tf_op jit(solution)/shard_map/ppermute | solution.py:177
  23.9 8.8 %collective-permute-start.3 = (bf16[512,768]{1,0:T(8,128)(2,1)S(1)}, bf16[512,768]{1,0:T(8,128)(2,1)}, u32[]{:S(2)}, u32[]{:S(2)}) collective-permute-start(bf16[512,768]{1,0:T(8,128)(2,1)S(1)} %collective-permute-done.1), channel_id=1, source_target_pairs={{0,8},{8,0},{16,24},{24,16},{1,9},{9,1},{17,25},{25,17},{2,10},{10... | collective-permute-start | bytes 2359304 | tf_op jit(solution)/shard_map/ppermute | solution.py:177
  23.9 8.7 %collective-permute-start = (bf16[64,2048]{1,0:T(8,128)(2,1)S(1)}, bf16[64,2048]{1,0:T(8,128)(2,1)S(1)}, u32[]{:S(2)}, u32[]{:S(2)}) collective-permute-start(bf16[64,2048]{1,0:T(8,128)(2,1)S(1)} %bitcast.36), channel_id=1, source_target_pairs={{0,16},{8,24},{16,0},{24,8},{1,17},{9,25},{17,1},{25,9},{2,18},{10... | collective-permute-start | bytes 786440 | tf_op jit(solution)/shard_map/ppermute | solution.py:174
  34.3 7.6 %copy-start.1 = (bf16[1,768,512]{2,1,0:T(8,128)(2,1)S(1)}, bf16[1,768,512]{2,1,0:T(8,128)(2,1)}, u32[]{:S(2)}) copy-start(bf16[1,768,512]{2,1,0:T(8,128)(2,1)} %param.9) | copy-start | bytes 2359300
  35.4 4.7 %collective-permute-start.4 = (bf16[128,384]{1,0:T(8,128)(2,1)S(1)}, bf16[128,384]{1,0:T(8,128)(2,1)S(1)}, u32[]{:S(2)}, u32[]{:S(2)}) collective-permute-start(bf16[128,384]{1,0:T(8,128)(2,1)S(1)} %project.1), channel_id=1, source_target_pairs={{0,16},{8,24},{16,0},{24,8},{1,17},{9,25},{17,1},{25,9},{2,18},{10... | collective-permute-start | bytes 294920 | tf_op jit(solution)/shard_map/ppermute | solution.py:174
  40.3 1.5 %collective-permute-start.5 = (bf16[128,768]{1,0:T(8,128)(2,1)S(1)}, bf16[128,768]{1,0:T(8,128)(2,1)S(1)}, u32[]{:S(2)}, u32[]{:S(2)}) collective-permute-start(bf16[128,768]{1,0:T(8,128)(2,1)S(1)} %bitcast.39), channel_id=1, source_target_pairs={{0,8},{8,0},{16,24},{24,16},{1,9},{9,1},{17,25},{25,17},{2,10},{10... | collective-permute-start | bytes 589832 | tf_op jit(solution)/shard_map/ppermute | solution.py:177

commit v2 on v1

--- a/solution.py
+++ b/solution.py
@@ -75,8 +75,12 @@
     )
 
 
-def whiten_kernel(scale, index_ref, hidden_ref, down_ref, factor_ref, out_ref, a_ref, u_ref, inverse_ref):
+def whiten_kernel(scale, index_ref, down_ref, *refs):
+    *row_refs, factor_ref, out_ref, hidden_ref, a_ref, u_ref, inverse_ref = refs
     width = hidden_ref.shape[1]
+    step = row_refs[0].shape[0]
+    for i, row_ref in enumerate(row_refs):
+        hidden_ref[i * step : (i + 1) * step, :] = row_ref[...]
     blocks = width // PANEL
     u_ref[...] = jnp.zeros_like(u_ref)
     for b in range(blocks):
@@ -109,7 +113,7 @@
     factor_ref[...] = u_ref[pl.ds(pl.multiple_of(index_ref[0] * share, 8), share), :]
 
 
-def whiten(index, hidden, down, share, slot_total):
+def whiten(index, rows, down, share, slot_total):
     width, columns = down.shape
     vmem = pl.BlockSpec(memory_space=pltpu.VMEM)
     return pl.pallas_call(
@@ -118,45 +122,52 @@
             jax.ShapeDtypeStruct((share, width), f32),
             jax.ShapeDtypeStruct((width, columns), f32),
         ),
-        in_specs=[pl.BlockSpec(memory_space=pltpu.SMEM), vmem, vmem],
+        in_specs=[pl.BlockSpec(memory_space=pltpu.SMEM), vmem] + [vmem] * len(rows),
         out_specs=(vmem, vmem),
         scratch_shapes=[
+            pltpu.VMEM((len(rows) * rows[0].shape[0], width), bf16),
             pltpu.VMEM((width, width), f32),
             pltpu.VMEM((width, width), f32),
             pltpu.VMEM((PANEL, PANEL), f32),
         ],
         compiler_params=pltpu.CompilerParams(vmem_limit_bytes=48 * 2**20),
         name="whiten",
-    )(index, hidden, down)
-
-
-def hidden_kernel(index_ref, token_ref, weight_ref, out_ref):
-    chunks, depth, both = weight_ref.shape
+    )(index, down, *rows)
+
+
+def project_kernel(index_ref, token_ref, *refs):
+    *weight_refs, out_ref = refs
+    chips, slots, both = out_ref.shape
     width = both // 2
-    total = None
-    for j in range(chunks):
-        at = pl.multiple_of(index_ref[j] * depth, depth)
-        part = jnp.dot(token_ref[:, pl.ds(at, depth)], weight_ref[j], preferred_element_type=f32)
-        total = part if total is None else total + part
-    gate, up = total[:, :width], total[:, width:]
-    hidden = (gate / (1.0 + jnp.exp(-gate)) * up).astype(bf16)
-    sources = chunks // CORES
-    rows = hidden.shape[0] // sources
-    for k in range(sources):
-        at = pl.multiple_of(index_ref[chunks + k] * rows, 16)
-        out_ref[pl.ds(at, rows), :] = hidden[k * rows : (k + 1) * rows]
-
-
-def project(chunk_index, tokens, weights):
+    depth = weight_refs[0].shape[0]
+    chip, core = index_ref[0], index_ref[1]
+    starts = [core * depth, (1 - core) * depth]
+    for k in range(chips):
+        owner = lax.rem(chip + k + 1, chips)
+        rows = pl.ds(pl.multiple_of(owner * slots, 16), slots)
+        for half in range(2):
+            total = None
+            for j in range(CORES):
+                part = jnp.dot(
+                    token_ref[rows, pl.ds(pl.multiple_of(starts[j], depth), depth)],
+                    weight_refs[2 * j + half][...],
+                    preferred_element_type=f32,
+                )
+                total = part if total is None else total + part
+            out_ref[k, :, half * width : (half + 1) * width] = total
+
+
+def project(index, tokens, weights, chips):
     vmem = pl.BlockSpec(memory_space=pltpu.VMEM)
+    both = 2 * weights[0].shape[1]
     return pl.pallas_call(
-        hidden_kernel,
-        out_shape=jax.ShapeDtypeStruct((tokens.shape[0], weights.shape[2] // 2), bf16),
-        in_specs=[pl.BlockSpec(memory_space=pltpu.SMEM), vmem, vmem],
+        project_kernel,
+        out_shape=jax.ShapeDtypeStruct((chips, tokens.shape[0] // chips, both), f32),
+        in_specs=[pl.BlockSpec(memory_space=pltpu.SMEM)] + [vmem] * (1 + len(weights)),
         out_specs=vmem,
         compiler_params=pltpu.CompilerParams(vmem_limit_bytes=48 * 2**20),
         name="project",
-    )(chunk_index, tokens, weights)
+    )(index, tokens, *weights)
 
 
 def body(tokens, expert_ids, gate_weight, up_weight, down_weight):
@@ -167,7 +178,7 @@
     dp = lax.axis_index("dp")
     chip, core = dp // CORES, dp % CORES
     width = gate_weight.shape[2]
-    share = width // chips
+    tok_rows, model = tokens.shape
 
     def to_chip(x, k):
         steps = [(i, (i + k * CORES) % dp_size) for i in range(dp_size)]
@@ -176,48 +187,47 @@
     def to_core(x):
         return lax.ppermute(x, "dp", [(i, i ^ 1) for i in range(dp_size)])
 
-    def weight_block(owner):
-        at = owner * share
-        return jnp.concatenate(
-            [
-                lax.dynamic_slice_in_dim(gate_weight[0], at, share, 1),
-                lax.dynamic_slice_in_dim(up_weight[0], at, share, 1),
-            ],
-            1,
-        )
-
-    blocks = [weight_block(chip)]
-    for k in range(1, chips):
-        blocks.append(to_chip(weight_block((chip + k) % chips), k))
-    sources = [(chip - k + chips) % chips for k in range(chips)]
-    blocks = blocks + [to_core(block) for block in blocks]
-    chunk_index = jnp.stack(
-        [source * CORES + core for source in sources]
-        + [source * CORES + 1 - core for source in sources]
-        + sources
-    ).astype(jnp.int32)
-
-    tok_rows = tokens.shape[0]
+    gate, up = gate_weight[0], up_weight[0]
+    weights = [gate, up, to_core(gate), to_core(up)]
+
     expert_range = jnp.arange(owners, dtype=jnp.int32)
     member = jnp.any(expert_ids[:, :, None] == expert_range[None, None, :], axis=1)
     earlier = (jnp.arange(tok_rows)[:, None] > jnp.arange(tok_rows)[None, :]).astype(jnp.int32)
     ranking = jnp.dot(earlier, member.astype(jnp.int32))
     slot_range = jnp.arange(CAP, dtype=jnp.int32)
     placing = (member[:, :, None] & (ranking[:, :, None] == slot_range[None, None, :])).astype(bf16)
-    outgoing = jnp.einsum("tec,td->ecd", placing, tokens, preferred_element_type=f32).astype(bf16)
-    arrived = lax.all_to_all(outgoing, "expert", split_axis=0, concat_axis=0, tiled=True)
-    received = arrived.reshape(-1, arrived.shape[-1])
-    slot_total = received.shape[0]
-
-    slots = jnp.concatenate([received] + [to_chip(received, k) for k in range(1, chips)], 0)
-    hidden = project(chunk_index, slots, jnp.stack(blocks))
-
-    pieces = jnp.stack([hidden] + [to_chip(hidden, k) for k in range(1, chips)])
-    ordered = jnp.roll(pieces[::-1], chip + 1, axis=0)
-    whole = jnp.moveaxis(ordered, 0, 1).reshape(chips * slot_total, width)
-    whole = jnp.concatenate([whole, to_core(whole)], 0)
+    outgoing = jnp.einsum(
+        "tec,tyd->yecd",
+        placing,
+        tokens.reshape(tok_rows, chips, model // chips),
+        preferred_element_type=f32,
+    ).astype(bf16)
+    groups = [
+        [(y * CORES + c) * experts + e for y in range(chips) for e in range(experts)]
+        for c in range(CORES)
+    ]
+    arrived = lax.all_to_all(
+        outgoing.reshape(chips * owners, CAP, model // chips),
+        ("dp", "expert"),
+        split_axis=0,
+        concat_axis=0,
+        axis_index_groups=groups,
+        tiled=True,
+    )
+    received = arrived.reshape(-1, model // chips)
+    slot_total = received.shape[0] // chips
+
+    index = jnp.stack([chip, core]).astype(jnp.int32)
+    partial = project(index, received, weights, chips)
+    total = partial[chips - 1]
+    for k in range(1, chips):
+        total = total + to_chip(partial[k - 1], k)
+    gate_sum, up_sum = total[:, :width], total[:, width:]
+    hidden = (gate_sum / (1.0 + jnp.exp(-gate_sum)) * up_sum).astype(bf16)
+    rows = [hidden] + [to_chip(hidden, k) for k in range(1, chips)]
+    rows = rows + [to_core(row) for row in rows]
     factor, whitened = whiten(
-        dp.astype(jnp.int32)[None], whole, down_weight[0], width // dp_size, slot_total
+        dp.astype(jnp.int32)[None], rows, down_weight[0], width // dp_size, slot_total
     )
     return (factor[None], whitened[None])
 

time: 71.3 us -> 69 us (0.968)
  other arithmetic: 3.74 us -> 0.88 us
  waiting for transfers between devices: 21 us -> 23.1 us
  starting transfers between devices: 12.4 us -> 10.9 us
  local copies, waits for them, and re-layouts: 1.66 us -> 0.77 us
    all_to_all x1, waiting for transfers between devices: 0.01 us -> 10 us  [body(): lax.all_to_all(outgoing.reshape(chips * owners, CAP, model // chips), ('d...]
    ppermute x3 -> x2, waiting for transfers between devices: 19.6 us -> 11.8 us  [to_chip(): return lax.ppermute(x, 'dp', steps)]
    ppermute x3 -> x2, starting transfers between devices: 6.52 us -> 2.05 us  [to_chip(): return lax.ppermute(x, 'dp', steps)]
    another operation x3 -> x1, other arithmetic: 2.62 us -> 0.08 us  [body(): index = jnp.stack([chip, core]).astype(jnp.int32)]
    all_to_all x1, starting transfers between devices: 5.81 us -> 8.29 us  [body(): lax.all_to_all(outgoing.reshape(chips * owners, CAP, model // chips), ('d...]
    dynamic_slice x1 -> x0, local copies, waits for them, and re-layouts: 1.52 us -> none  [weight_block(): lax.dynamic_slice_in_dim(up_weight[0], at, share, 1)]
    concatenate x3 -> x0, other arithmetic: 1.01 us -> none  [the longest x1 0.94 us: weight_block(): jnp.concatenate([lax.dynamic_slice_in_dim(gate_weight[0], at, share, 1),...]
    convert_element_type x0 -> x1, local copies, waits for them, and re-layouts: none -> 0.73 us  [body(): outgoing = jnp.einsum('tec,tyd->yecd', placing, tokens.reshape(tok_rows,...]
  transfers between devices with their start and end apart: 7 -> 7, of which waited for: 4 -> 4; matrix products, arithmetic and copies ran while one was open for 3% -> 4% of each run, Pallas kernels for 0% -> 0%
where the time goes in v2:
time: 69 us; the launch traced here: 68.7 us
  Pallas kernels  31 us (45%)
  waiting for transfers between devices  23.1 us (33%)
  starting transfers between devices  10.9 us (16%)
  matrix products  1.3 us (2%)
  other arithmetic  0.88 us (1%)
  local copies, waits for them, and re-layouts  0.77 us (1%)
  between operations  0.73 us (1%)
    pallas_call x1, Pallas kernels, whiten(): pl.pallas_call(functools.partial(whiten_kernel, 1.0 / slot_total), out_sh...  29.2 us
    ppermute x2, waiting for transfers between devices, to_chip(): return lax.ppermute(x, 'dp', steps)  11.8 us
    all_to_all x1, waiting for transfers between devices, body(): lax.all_to_all(outgoing.reshape(chips * owners, CAP, model // chips), ('d...  10 us
    all_to_all x1, starting transfers between devices, body(): lax.all_to_all(outgoing.reshape(chips * owners, CAP, model // chips), ('d...  8.29 us
    ppermute x2, starting transfers between devices, to_chip(): return lax.ppermute(x, 'dp', steps)  2.05 us
    pallas_call x1, Pallas kernels, project(): pl.pallas_call(project_kernel, out_shape=jax.ShapeDtypeStruct((chips, tok...  1.75 us
  transfers between devices with their start and end apart: 7, of which 4 were waited for; matrix products, arithmetic and copies ran while one was open for 4% of the time, Pallas kernels for 0%

profile of v2, /device:TPU:0, one launch (start us, length us, event | category | flops | bytes accessed | tf_op | source)
XLA Modules:
  0.0 68.7 jit_solution(6279039208542342456)
XLA Ops:
  0.6 0.0 copy-start
  0.6 0.0 copy-start.1
  0.7 0.5 collective-permute-start
  1.2 0.1 collective-permute-start.1
  1.2 0.7 %fusion.4 = pred[64,8]{0,1:T(8,128)(4,1)S(1)} fusion(s32[64,8]{0,1:T(8,128)} %param.6), kind=kLoop, calls=%fused_computation.12 | loop fusion | flops 7680 | bytes 2560 | tf_op jit(solution)/shard_map/reduce_or | solution.py:194
  1.9 0.1 fusion.5
  2.1 1.2 %fusion = bf16[2,8,8,1024]{3,2,0,1:T(8,128)(2,1)S(1)} fusion(bf16[8,2,8,1024]{3,2,1,0:T(8,128)(2,1)} %bitcast.38, s32[64,8]{0,1:T(8,128)S(1)} %fusion.5, pred[64,8]{0,1:T(8,128)(4,1)S(1)} %fusion.4), kind=kOutput, calls=%fused_computation.1 | convolution fusion | flops 16916480 | bytes 526848 | tf_op jit(solution)/shard_map/tec,tyd->yecd/dot_general | solution.py:199
  3.3 0.7 %copy.13 = bf16[2,8,8,1024]{3,2,1,0:T(8,128)(2,1)} copy(bf16[2,8,8,1024]{3,2,0,1:T(8,128)(2,1)S(1)} %fusion) | data formatting | bytes 524288 | tf_op jit(solution)/shard_map/convert_element_type | solution.py:204
  4.0 8.3 %all-to-all-start = ((bf16[16,8,1024]{2,1,0:T(8,128)(2,1)}), bf16[16,8,1024]{2,1,0:T(8,128)(2,1)S(1)}, u32[]{:S(2)}, u32[]{:S(2)}) async-start(bf16[16,8,1024]{2,1,0:T(8,128)(2,1)} %bitcast.37), calls=%async_computation | async-start | bytes 524288 | tf_op jit(solution)/shard_map/all_to_all | solution.py:209
  12.3 0.1 pad_add_fusion.index_ref
  12.4 10.0 %all-to-all-done = bf16[16,8,1024]{2,1,0:T(8,128)(2,1)S(1)} async-done(((bf16[16,8,1024]{2,1,0:T(8,128)(2,1)}), bf16[16,8,1024]{2,1,0:T(8,128)(2,1)S(1)}, u32[]{:S(2)}, u32[]{:S(2)}) %all-to-all-start) | async-done | bytes 262176 | tf_op jit(solution)/shard_map/all_to_all | solution.py:209
  22.4 0.0 collective-permute-done.refs_2_
  22.4 0.0 collective-permute-done.1.refs_3_
  22.4 0.0 copy-done
  22.4 0.0 copy-done.1
  22.4 1.7 %project.1 = f32[2,64,1536]{2,1,0:T(8,128)S(1)} custom-call(s32[2]{0:T(128)S(1)} %pad_add_fusion.index_ref, bf16[128,1024]{1,0:T(8,128)(2,1)S(1)} %bitcast.31, bf16[512,768]{1,0:T(8,128)(2,1)S(1)} %bitcast.33, bf16[512,768]{1,0:T(8,128)(2,1)S(1)} %bitcast.35, bf16[512,768]{1,0:T(8,128)(2,1)S(1)} %collective-permute-done.refs_2_, ...), custom_call_target="tpu_custom_call" | custom-call | tf_op jit(solution)/shard_map/project/pallas_call | solution.py:163
  24.2 0.0 copy-start.2
  24.2 1.2 %collective-permute-start.2 = (f32[64,1536]{1,0:T(8,128)S(1)}, f32[64,1536]{1,0:T(8,128)S(1)}, u32[]{:S(2)}, u32[]{:S(2)}) collective-permute-start(f32[64,1536]{1,0:T(8,128)S(1)} %slice_bitcast_fusion), channel_id=1, source_target_pairs={{0,16},{8,24},{16,0},{24,8},{1,17},{9,25},{17,1},{25,9},{2,18},{10... | collective-permute-start | bytes 1179656 | tf_op jit(solution)/shard_map/ppermute | solution.py:185
  25.4 8.0 %collective-permute-done.2 = f32[64,1536]{1,0:T(8,128)S(1)} collective-permute-done((f32[64,1536]{1,0:T(8,128)S(1)}, f32[64,1536]{1,0:T(8,128)S(1)}, u32[]{:S(2)}, u32[]{:S(2)}) %collective-permute-start.2) | collective-permute-done | bytes 393248 | tf_op jit(solution)/shard_map/ppermute | solution.py:185
  33.4 0.1 fusion.3.refs_0_
  33.5 0.9 %collective-permute-start.3 = (bf16[64,768]{1,0:T(8,128)(2,1)S(1)}, bf16[64,768]{1,0:T(8,128)(2,1)S(1)}, u32[]{:S(2)}, u32[]{:S(2)}) collective-permute-start(bf16[64,768]{1,0:T(8,128)(2,1)S(1)} %fusion.3.refs_0_), channel_id=1, source_target_pairs={{0,16},{8,24},{16,0},{24,8},{1,17},{9,25},{17,1},{25,9},{2,18},{10... | collective-permute-start | bytes 294920 | tf_op jit(solution)/shard_map/ppermute | solution.py:185
  34.4 0.0 collective-permute-start.4
  34.4 3.8 %collective-permute-done.3.refs_1_ = bf16[64,768]{1,0:T(8,128)(2,1)S(1)} collective-permute-done((bf16[64,768]{1,0:T(8,128)(2,1)S(1)}, bf16[64,768]{1,0:T(8,128)(2,1)S(1)}, u32[]{:S(2)}, u32[]{:S(2)}) %collective-permute-start.3) | collective-permute-done | bytes 98336 | tf_op jit(solution)/shard_map/ppermute | solution.py:185
  38.2 0.0 collective-permute-start.5
  38.2 0.0 collective-permute-done.4.refs_2_
  38.2 1.3 %collective-permute-done.5.refs_3_ = bf16[64,768]{1,0:T(8,128)(2,1)S(1)} collective-permute-done((bf16[64,768]{1,0:T(8,128)(2,1)S(1)}, bf16[64,768]{1,0:T(8,128)(2,1)S(1)}, u32[]{:S(2)}, u32[]{:S(2)}) %collective-permute-start.5) | collective-permute-done | bytes 98336 | tf_op jit(solution)/shard_map/ppermute | solution.py:188
  39.5 0.0 copy-done.2
  39.5 29.2 %whiten.1 = (f32[192,768]{1,0:T(8,128)}, f32[768,512]{1,0:T(8,128)}) custom-call(s32[1]{0:T(128)} %bitcast.index_ref, bf16[768,512]{1,0:T(8,128)(2,1)S(1)} %bitcast.36, bf16[64,768]{1,0:T(8,128)(2,1)S(1)} %fusion.3.refs_0_, bf16[64,768]{1,0:T(8,128)(2,1)S(1)} %collective-permute-done.3.refs_1_, bf16[64,768]{1,0:T(8,128)(2,1)S(1)} %collective-permute-done.4.refs_2_, ...), custom_call_target="tpu_custom_call" | custom-call | tf_op jit(solution)/shard_map/whiten/pallas_call | solution.py:119
  (2 shorter events, 0.1 us)
Async XLA Ops:
  0.6 21.8 %copy-start = (bf16[1,512,768]{2,1,0:T(8,128)(2,1)S(1)}, bf16[1,512,768]{2,1,0:T(8,128)(2,1)}, u32[]{:S(2)}) copy-start(bf16[1,512,768]{2,1,0:T(8,128)(2,1)} %param.7) | copy-start | bytes 2359300
  0.6 21.8 %copy-start.1 = (bf16[1,512,768]{2,1,0:T(8,128)(2,1)S(1)}, bf16[1,512,768]{2,1,0:T(8,128)(2,1)}, u32[]{:S(2)}) copy-start(bf16[1,512,768]{2,1,0:T(8,128)(2,1)} %param.8) | copy-start | bytes 2359300
  0.7 21.7 %collective-permute-start = (bf16[512,768]{1,0:T(8,128)(2,1)}, bf16[512,768]{1,0:T(8,128)(2,1)S(1)}, u32[]{:S(2)}, u32[]{:S(2)}) collective-permute-start(bf16[512,768]{1,0:T(8,128)(2,1)} %bitcast.32), channel_id=1, source_target_pairs={{0,8},{8,0},{16,24},{24,16},{1,9},{9,1},{17,25},{25,17},{2,10},{10... | collective-permute-start | bytes 2359304 | tf_op jit(solution)/shard_map/ppermute | solution.py:188
  1.2 21.2 %collective-permute-start.1 = (bf16[512,768]{1,0:T(8,128)(2,1)}, bf16[512,768]{1,0:T(8,128)(2,1)S(1)}, u32[]{:S(2)}, u32[]{:S(2)}) collective-permute-start(bf16[512,768]{1,0:T(8,128)(2,1)} %bitcast.34), channel_id=1, source_target_pairs={{0,8},{8,0},{16,24},{24,16},{1,9},{9,1},{17,25},{25,17},{2,10},{10... | collective-permute-start | bytes 2359304 | tf_op jit(solution)/shard_map/ppermute | solution.py:188
  4.0 18.4 %all-to-all-start = ((bf16[16,8,1024]{2,1,0:T(8,128)(2,1)}), bf16[16,8,1024]{2,1,0:T(8,128)(2,1)S(1)}, u32[]{:S(2)}, u32[]{:S(2)}) async-start(bf16[16,8,1024]{2,1,0:T(8,128)(2,1)} %bitcast.37), calls=%async_computation | async-start | bytes 524288 | tf_op jit(solution)/shard_map/all_to_all | solution.py:209
  24.2 15.3 %copy-start.2 = (bf16[1,768,512]{2,1,0:T(8,128)(2,1)S(1)}, bf16[1,768,512]{2,1,0:T(8,128)(2,1)}, u32[]{:S(2)}) copy-start(bf16[1,768,512]{2,1,0:T(8,128)(2,1)} %param.9) | copy-start | bytes 2359300
  24.2 9.2 %collective-permute-start.2 = (f32[64,1536]{1,0:T(8,128)S(1)}, f32[64,1536]{1,0:T(8,128)S(1)}, u32[]{:S(2)}, u32[]{:S(2)}) collective-permute-start(f32[64,1536]{1,0:T(8,128)S(1)} %slice_bitcast_fusion), channel_id=1, source_target_pairs={{0,16},{8,24},{16,0},{24,8},{1,17},{9,25},{17,1},{25,9},{2,18},{10... | collective-permute-start | bytes 1179656 | tf_op jit(solution)/shard_map/ppermute | solution.py:185
  33.5 4.7 %collective-permute-start.3 = (bf16[64,768]{1,0:T(8,128)(2,1)S(1)}, bf16[64,768]{1,0:T(8,128)(2,1)S(1)}, u32[]{:S(2)}, u32[]{:S(2)}) collective-permute-start(bf16[64,768]{1,0:T(8,128)(2,1)S(1)} %fusion.3.refs_0_), channel_id=1, source_target_pairs={{0,16},{8,24},{16,0},{24,8},{1,17},{9,25},{17,1},{25,9},{2,18},{10... | collective-permute-start | bytes 294920 | tf_op jit(solution)/shard_map/ppermute | solution.py:185
  34.4 3.8 %collective-permute-start.4 = (bf16[64,768]{1,0:T(8,128)(2,1)S(1)}, bf16[64,768]{1,0:T(8,128)(2,1)S(1)}, u32[]{:S(2)}, u32[]{:S(2)}) collective-permute-start(bf16[64,768]{1,0:T(8,128)(2,1)S(1)} %fusion.3.refs_0_), channel_id=1, source_target_pairs={{0,8},{8,0},{16,24},{24,16},{1,9},{9,1},{17,25},{25,17},{2,10},{10... | collective-permute-start | bytes 294920 | tf_op jit(solution)/shard_map/ppermute | solution.py:188
  38.2 1.3 %collective-permute-start.5 = (bf16[64,768]{1,0:T(8,128)(2,1)S(1)}, bf16[64,768]{1,0:T(8,128)(2,1)S(1)}, u32[]{:S(2)}, u32[]{:S(2)}) collective-permute-start(bf16[64,768]{1,0:T(8,128)(2,1)S(1)} %collective-permute-done.3.refs_1_), channel_id=1, source_target_pairs={{0,8},{8,0},{16,24},{24,16},{1,9},{9,1},{17,25},{25,17},{2,10},{10... | collective-permute-start | bytes 294920 | tf_op jit(solution)/shard_map/ppermute | solution.py:188

commit v3 on v2

--- a/solution.py
+++ b/solution.py
@@ -11,6 +11,8 @@
 CORES = 2
 PANEL = 128
 WINDOW = 16
+SUPER = 64
+CHUNK = 256
 damping = 0.02
 highest = lax.Precision.HIGHEST
 f32 = jnp.float32
@@ -18,62 +20,96 @@
 
 
 def reciprocal(value):
-    guess = pl.reciprocal(value, approx=True)
-    return guess * (2.0 - value * guess)
-
-
-def factor_block(a_ref, u_ref, inverse_ref, start):
-    row_in_window = lax.broadcasted_iota(jnp.int32, (WINDOW, PANEL), 0)
-    lane = lax.broadcasted_iota(jnp.int32, (WINDOW, PANEL), 1)
+    return pl.reciprocal(value, approx=True)
+
+
+def transposed_dot(a, b, precision=None):
+    return lax.dot_general(a, b, (((0,), (0,)), ((), ())), preferred_element_type=f32, precision=precision)
+
+def tree(terms):
+    while len(terms) > 1:
+        terms = [terms[i] + terms[i + 1] if i + 1 < len(terms) else terms[i] for i in range(0, len(terms), 2)]
+    return terms[0]
+
+def eliminate(columns, sides):
+    row8 = lax.broadcasted_iota(jnp.int32, (8, PANEL), 0)
+    groups = WINDOW // 8
+    uppers = [[jnp.zeros((8, PANEL), f32) for _ in range(groups)] for _ in sides]
+    sides = [list(side) for side in sides]
+    scales = []
+    for r in range(0, WINDOW, 2):
+        h, t = r // 8, r % 8
+        first, second = columns[r], columns[r + 1]
+        a, b, c = first[h][t : t + 1], first[h][t + 1 : t + 2], second[h][t + 1 : t + 2]
+        det = a * c - b * b
+        q = reciprocal(det)
+        root_a = lax.rsqrt(a)
+        inv_a = root_a * root_a
+        root_d = lax.rsqrt(det * inv_a)
+        slope = b * inv_a
+        scales.append((a * q, b * q, c * q))
+        l0, l1 = [], []
+        pair = (row8 == t) | (row8 == t + 1)
+        for g in range(groups):
+            f, d = first[g], second[g]
+            if g == h:
+                f, d = jnp.where(pair, 0.0, f), jnp.where(pair, 0.0, d)
+            l0.append((c * f - b * d) * q)
+            l1.append((a * d - b * f) * q)
+        for j in range(r + 2, WINDOW):
+            x, y = columns[j][h][t : t + 1], columns[j][h][t + 1 : t + 2]
+            columns[j] = [columns[j][g] - (l0[g] * x + l1[g] * y) for g in range(groups)]
+        for n, side in enumerate(sides):
+            x, y = side[h][t : t + 1], side[h][t + 1 : t + 2]
+            uppers[n][h] = jnp.where(row8 == t, x * root_a, jnp.where(row8 == t + 1, (y - slope * x) * root_d, uppers[n][h]))
+            sides[n] = [side[g] - (l0[g] * x + l1[g] * y) for g in range(groups)]
+    solved = []
+    for side in sides:
+        rows = []
+        for r in range(0, WINDOW, 2):
+            h, t = r // 8, r % 8
+            aq, bq, cq = scales[r // 2]
+            x, y = side[h][t : t + 1], side[h][t + 1 : t + 2]
+            rows += [cq * x - bq * y, aq * y - bq * x]
+        solved.append(rows)
+    return uppers, solved
+
+def factor_steps(block, result, zero):
     lane8 = lax.broadcasted_iota(jnp.int32, (8, PANEL), 1)
     row8 = lax.broadcasted_iota(jnp.int32, (8, PANEL), 0)
     groups = PANEL // 8
     per_window = WINDOW // 8
-    left = [a_ref[start + 8 * i : start + 8 * i + 8, start : start + PANEL] for i in range(groups)]
+    left = [block[8 * i : 8 * i + 8] for i in range(groups)]
     right = [(lane8 == row8 + 8 * i).astype(f32) for i in range(groups)]
+    uppers, inverses = [], []
     for window in range(PANEL // WINDOW):
         k = window * WINDOW
         first = window * per_window
-        rows_l = jnp.concatenate(left[first : first + per_window], 0)
-        rows_r = jnp.concatenate(right[first : first + per_window], 0)
-        columns = [
-            jnp.broadcast_to(rows_l[:, k + c : k + c + 1], (WINDOW, PANEL)) for c in range(WINDOW)
-        ]
-        upper_l = jnp.zeros((WINDOW, PANEL), f32)
-        upper_r = jnp.zeros((WINDOW, PANEL), f32)
-        pivots = jnp.zeros((WINDOW, PANEL), f32)
-        for r in range(WINDOW):
-            here = row_in_window == r
-            pivot = columns[r][r : r + 1, :]
-            ratio = jnp.where(here, 0.0, columns[r]) * reciprocal(pivot)
-            pivot_l, pivot_r = rows_l[r : r + 1, :], rows_r[r : r + 1, :]
-            upper_l = jnp.where(here, pivot_l, upper_l)
-            upper_r = jnp.where(here, pivot_r, upper_r)
-            pivots = jnp.where(here, pivot, pivots)
-            rows_l = rows_l - ratio * pivot_l
-            rows_r = rows_r - ratio * pivot_r
-            for c in range(r + 1, WINDOW):
-                columns[c] = columns[c] - ratio * columns[c][r : r + 1, :]
-        inverse, root = reciprocal(pivots), lax.rsqrt(pivots)
-        rows_l, rows_r = rows_l * inverse, rows_r * inverse
-        u_ref[start + k : start + k + WINDOW, start : start + PANEL] = jnp.where(
-            lane >= row_in_window + k, upper_l * root, 0.0
-        )
-        inverse_ref[k : k + WINDOW, :] = upper_r * root
-        for i in range(first + per_window, groups):
-            old, new_l, new_r = left[i], left[i], right[i]
-            for c in range(WINDOW):
-                scale = jnp.broadcast_to(old[:, k + c : k + c + 1], (8, PANEL))
-                new_l = new_l - scale * rows_l[c : c + 1, :]
-                new_r = new_r - scale * rows_r[c : c + 1, :]
-            left[i], right[i] = new_l, new_r
-
-
-def transposed_dot(a, b, precision=None):
-    return lax.dot_general(
-        a, b, (((0,), (0,)), ((), ())), preferred_element_type=f32, precision=precision
-    )
-
+        mine = range(first, first + per_window)
+        columns = [[jnp.broadcast_to(left[g][:, k + c : k + c + 1], (8, PANEL)) + zero for g in mine] for c in range(WINDOW)]
+        (up_l, up_r), (w_l, w_r) = eliminate(columns, [[left[g] for g in mine], [right[g] for g in mine]])
+        uppers += [jnp.where(lane8 >= row8 + 8 * g, u, 0.0) for g, u in zip(mine, up_l)]
+        inverses += up_r
+        near = min(groups, (k // SUPER + 1) * SUPER // 8)
+        for i in range(first + per_window, near):
+            scale = [jnp.broadcast_to(left[i][:, k + c : k + c + 1], (8, PANEL)) for c in range(WINDOW)]
+            left[i] = left[i] - tree([scale[c] * w_l[c] for c in range(WINDOW)])
+            right[i] = right[i] - tree([scale[c] * w_r[c] for c in range(WINDOW)])
+        if (k + WINDOW) % SUPER == 0 and near < groups:
+            parts = SUPER // 8
+            up = jnp.concatenate(uppers[-parts:], 0)
+            inv = jnp.concatenate(inverses[-parts:], 0)
+            mult = up[:, near * 8 :]
+            chg_l = transposed_dot(mult, up, highest)
+            chg_r = transposed_dot(mult, inv, highest)
+            for i in range(near, groups):
+                o = (i - near) * 8
+                left[i] = left[i] - chg_l[o : o + 8]
+                right[i] = right[i] - chg_r[o : o + 8]
+        if window == PANEL // WINDOW - 1:
+            result.append(jnp.concatenate(uppers, 0))
+            result.append(jnp.concatenate(inverses, 0))
+        yield
 
 def whiten_kernel(scale, index_ref, down_ref, *refs):
     *row_refs, factor_ref, out_ref, hidden_ref, a_ref, u_ref, inverse_ref = refs
@@ -82,53 +118,84 @@
     for i, row_ref in enumerate(row_refs):
         hidden_ref[i * step : (i + 1) * step, :] = row_ref[...]
     blocks = width // PANEL
-    u_ref[...] = jnp.zeros_like(u_ref)
-    for b in range(blocks):
+    steps = PANEL // WINDOW
+    zero = jnp.full((8, PANEL), jnp.where(index_ref[0] < 0, 1.0, 0.0), f32)
+
+    def gram(b, lo, hi):
         s = b * PANEL
-        gram = transposed_dot(hidden_ref[:, s : s + PANEL], hidden_ref[:, s:]) * scale
-        row = lax.broadcasted_iota(jnp.int32, gram.shape, 0)
-        lane = lax.broadcasted_iota(jnp.int32, gram.shape, 1)
-        a_ref[s : s + PANEL, s:] = jnp.where(row == lane, gram + damping, gram)
-    for p in range(blocks):
+        g = transposed_dot(hidden_ref[:, s : s + PANEL], hidden_ref[:, lo:hi]) * scale
+        row = lax.broadcasted_iota(jnp.int32, g.shape, 0) + s
+        lane = lax.broadcasted_iota(jnp.int32, g.shape, 1) + lo
+        return jnp.where(row == lane, g + damping, g)
+
+    def chunks(start):
+        return [(c, min(c + CHUNK, width)) for c in range(start, width, CHUNK)]
+
+    def store_gram(b, lo, hi):
+        a_ref[b * PANEL : (b + 1) * PANEL, lo:hi] = gram(b, lo, hi)
+
+    def panel(p, lo, hi):
         s, e = p * PANEL, (p + 1) * PANEL
-        factor_block(a_ref, u_ref, inverse_ref, s)
-        if e < width:
-            panel = jnp.dot(
-                inverse_ref[...], a_ref[s:e, e:], preferred_element_type=f32, precision=highest
-            )
-            u_ref[s:e, e:] = panel
-            for b in range(p + 1, blocks):
-                t = b * PANEL
-                a_ref[t : t + PANEL, t:] = a_ref[t : t + PANEL, t:] - transposed_dot(
-                    panel[:, t - e : t - e + PANEL], panel[:, t - e :], highest
-                )
+        u_ref[s:e, lo:hi] = jnp.dot(inverse_ref[p % 2], a_ref[s:e, lo:hi], preferred_element_type=f32, precision=highest)
+
+    def trail(p, b, lo, hi):
+        s, e, t = p * PANEL, (p + 1) * PANEL, b * PANEL
+        a_ref[t : t + PANEL, lo:hi] = a_ref[t : t + PANEL, lo:hi] - transposed_dot(u_ref[s:e, t : t + PANEL], u_ref[s:e, lo:hi], highest)
+
+    def output(p):
+        s, e = p * PANEL, (p + 1) * PANEL
         rows = u_ref[s:e, s:]
         high = rows.astype(bf16)
         low = (rows - high.astype(f32)).astype(bf16)
         down = down_ref[s:, :]
-        out_ref[s:e, :] = jnp.dot(high, down, preferred_element_type=f32) + jnp.dot(
-            low, down, preferred_element_type=f32
-        )
+        out_ref[s:e, :] = jnp.dot(high, down, preferred_element_type=f32) + jnp.dot(low, down, preferred_element_type=f32)
+
+    def clear(p):
+        if p: u_ref[p * PANEL : (p + 1) * PANEL, : p * PANEL] = jnp.zeros((PANEL, p * PANEL), f32)
+
+    block = gram(0, 0, PANEL)
+    work = [functools.partial(store_gram, 0, lo, hi) for lo, hi in chunks(PANEL)]
+    for b in range(1, blocks):
+        work += [functools.partial(store_gram, b, lo, hi) for lo, hi in chunks(b * PANEL)]
+        work.append(functools.partial(clear, b))
+    for p in range(blocks):
+        s, e = p * PANEL, (p + 1) * PANEL
+        result = []
+        done = 0
+        for i, _ in enumerate(factor_steps(block, result, zero)):
+            upto = len(work) * (i + 1) // steps
+            for job in work[done:upto]: job()
+            done = upto
+        u_ref[s:e, s:e] = result[0]
+        if e < width:
+            inverse_ref[p % 2] = result[1]
+            nxt = jnp.dot(result[1], a_ref[s:e, e:e+PANEL], preferred_element_type=f32, precision=highest)
+            u_ref[s:e, e:e+PANEL] = nxt
+            block = a_ref[e:e+PANEL, e:e+PANEL] - transposed_dot(nxt, nxt, highest)
+            f = e + PANEL
+            work = [functools.partial(panel, p, lo, hi) for lo, hi in chunks(f)]
+            work += [functools.partial(trail, p, p + 1, lo, hi) for lo, hi in chunks(f)]
+            for b in range(p + 2, blocks):
+                work += [functools.partial(trail, p, b, lo, hi) for lo, hi in chunks(b * PANEL)]
+            work.append(functools.partial(output, p))
+        else:
+            output(p)
     share = factor_ref.shape[0]
     factor_ref[...] = u_ref[pl.ds(pl.multiple_of(index_ref[0] * share, 8), share), :]
-
 
 def whiten(index, rows, down, share, slot_total):
     width, columns = down.shape
     vmem = pl.BlockSpec(memory_space=pltpu.VMEM)
     return pl.pallas_call(
         functools.partial(whiten_kernel, 1.0 / slot_total),
-        out_shape=(
-            jax.ShapeDtypeStruct((share, width), f32),
-            jax.ShapeDtypeStruct((width, columns), f32),
-        ),
+        out_shape=(jax.ShapeDtypeStruct((share, width), f32), jax.ShapeDtypeStruct((width, columns), f32)),
         in_specs=[pl.BlockSpec(memory_space=pltpu.SMEM), vmem] + [vmem] * len(rows),
         out_specs=(vmem, vmem),
         scratch_shapes=[
             pltpu.VMEM((len(rows) * rows[0].shape[0], width), bf16),
             pltpu.VMEM((width, width), f32),
             pltpu.VMEM((width, width), f32),
-            pltpu.VMEM((PANEL, PANEL), f32),
+            pltpu.VMEM((2, PANEL, PANEL), f32),
         ],
         compiler_params=pltpu.CompilerParams(vmem_limit_bytes=48 * 2**20),
         name="whiten",

time: 69 us -> 59.8 us (0.87)
  Pallas kernels: 31 us -> 21.8 us
    pallas_call x1, Pallas kernels: 29.2 us -> 20.1 us  [whiten(): pl.pallas_call(functools.partial(whiten_kernel, 1.0 / slot_total), out_sh...]
  transfers between devices with their start and end apart: 7 -> 7, of which waited for: 4 -> 4; matrix products, arithmetic and copies ran while one was open for 4% -> 5% of each run, Pallas kernels for 0% -> 0%
where the time goes in v3:
time: 59.8 us; the launch traced here: 59.5 us
  waiting for transfers between devices  23.1 us (39%)
  Pallas kernels  21.8 us (36%)
  starting transfers between devices  10.9 us (18%)
  matrix products  1.3 us (2%)
  other arithmetic  0.88 us (1%)
  local copies, waits for them, and re-layouts  0.77 us (1%)
  between operations  0.73 us (1%)
    pallas_call x1, Pallas kernels, whiten(): pl.pallas_call(functools.partial(whiten_kernel, 1.0 / slot_total), out_sh...  20.1 us
    ppermute x2, waiting for transfers between devices, to_chip(): return lax.ppermute(x, 'dp', steps)  11.8 us
    all_to_all x1, waiting for transfers between devices, body(): lax.all_to_all(outgoing.reshape(chips * owners, CAP, model // chips), ('d...  10 us
    all_to_all x1, starting transfers between devices, body(): lax.all_to_all(outgoing.reshape(chips * owners, CAP, model // chips), ('d...  8.29 us
    ppermute x2, starting transfers between devices, to_chip(): return lax.ppermute(x, 'dp', steps)  2.05 us
    pallas_call x1, Pallas kernels, project(): pl.pallas_call(project_kernel, out_shape=jax.ShapeDtypeStruct((chips, tok...  1.75 us
    ppermute x4, waiting for transfers between devices, to_core(): return lax.ppermute(x, 'dp', [(i, i ^ 1) for i in range(dp_size)])  1.3 us
  transfers between devices with their start and end apart: 7, of which 4 were waited for; matrix products, arithmetic and copies ran while one was open for 5% of the time, Pallas kernels for 0%

profile of v3, /device:TPU:0, one launch (start us, length us, event | category | flops | bytes accessed | tf_op | source)
XLA Modules:
  0.0 59.5 jit_solution(8187514727958754076)
XLA Ops:
  0.6 0.0 copy-start
  0.6 0.0 copy-start.1
  0.7 0.5 collective-permute-start
  1.2 0.1 collective-permute-start.1
  1.2 0.7 %fusion.4 = pred[64,8]{0,1:T(8,128)(4,1)S(1)} fusion(s32[64,8]{0,1:T(8,128)} %param.6), kind=kLoop, calls=%fused_computation.12 | loop fusion | flops 7680 | bytes 2560 | tf_op jit(solution)/shard_map/reduce_or | solution.py:261
  1.9 0.1 fusion.5
  2.1 1.2 %fusion = bf16[2,8,8,1024]{3,2,0,1:T(8,128)(2,1)S(1)} fusion(bf16[8,2,8,1024]{3,2,1,0:T(8,128)(2,1)} %bitcast.38, s32[64,8]{0,1:T(8,128)S(1)} %fusion.5, pred[64,8]{0,1:T(8,128)(4,1)S(1)} %fusion.4), kind=kOutput, calls=%fused_computation.1 | convolution fusion | flops 16916480 | bytes 526848 | tf_op jit(solution)/shard_map/tec,tyd->yecd/dot_general | solution.py:266
  3.3 0.7 %copy.13 = bf16[2,8,8,1024]{3,2,1,0:T(8,128)(2,1)} copy(bf16[2,8,8,1024]{3,2,0,1:T(8,128)(2,1)S(1)} %fusion) | data formatting | bytes 524288 | tf_op jit(solution)/shard_map/convert_element_type | solution.py:271
  4.0 8.3 %all-to-all-start = ((bf16[16,8,1024]{2,1,0:T(8,128)(2,1)}), bf16[16,8,1024]{2,1,0:T(8,128)(2,1)S(1)}, u32[]{:S(2)}, u32[]{:S(2)}) async-start(bf16[16,8,1024]{2,1,0:T(8,128)(2,1)} %bitcast.37), calls=%async_computation | async-start | bytes 524288 | tf_op jit(solution)/shard_map/all_to_all | solution.py:276
  12.3 0.1 pad_add_fusion.index_ref
  12.4 10.0 %all-to-all-done = bf16[16,8,1024]{2,1,0:T(8,128)(2,1)S(1)} async-done(((bf16[16,8,1024]{2,1,0:T(8,128)(2,1)}), bf16[16,8,1024]{2,1,0:T(8,128)(2,1)S(1)}, u32[]{:S(2)}, u32[]{:S(2)}) %all-to-all-start) | async-done | bytes 262176 | tf_op jit(solution)/shard_map/all_to_all | solution.py:276
  22.4 0.0 collective-permute-done.refs_2_
  22.4 0.0 collective-permute-done.1.refs_3_
  22.4 0.0 copy-done
  22.4 0.0 copy-done.1
  22.4 1.7 %project.1 = f32[2,64,1536]{2,1,0:T(8,128)S(1)} custom-call(s32[2]{0:T(128)S(1)} %pad_add_fusion.index_ref, bf16[128,1024]{1,0:T(8,128)(2,1)S(1)} %bitcast.31, bf16[512,768]{1,0:T(8,128)(2,1)S(1)} %bitcast.33, bf16[512,768]{1,0:T(8,128)(2,1)S(1)} %bitcast.35, bf16[512,768]{1,0:T(8,128)(2,1)S(1)} %collective-permute-done.refs_2_, ...), custom_call_target="tpu_custom_call" | custom-call | tf_op jit(solution)/shard_map/project/pallas_call | solution.py:230
  24.2 0.0 copy-start.2
  24.2 1.2 %collective-permute-start.2 = (f32[64,1536]{1,0:T(8,128)S(1)}, f32[64,1536]{1,0:T(8,128)S(1)}, u32[]{:S(2)}, u32[]{:S(2)}) collective-permute-start(f32[64,1536]{1,0:T(8,128)S(1)} %slice_bitcast_fusion), channel_id=1, source_target_pairs={{0,16},{8,24},{16,0},{24,8},{1,17},{9,25},{17,1},{25,9},{2,18},{10... | collective-permute-start | bytes 1179656 | tf_op jit(solution)/shard_map/ppermute | solution.py:252
  25.4 8.0 %collective-permute-done.2 = f32[64,1536]{1,0:T(8,128)S(1)} collective-permute-done((f32[64,1536]{1,0:T(8,128)S(1)}, f32[64,1536]{1,0:T(8,128)S(1)}, u32[]{:S(2)}, u32[]{:S(2)}) %collective-permute-start.2) | collective-permute-done | bytes 393248 | tf_op jit(solution)/shard_map/ppermute | solution.py:252
  33.4 0.1 fusion.3.refs_0_
  33.5 0.9 %collective-permute-start.3 = (bf16[64,768]{1,0:T(8,128)(2,1)S(1)}, bf16[64,768]{1,0:T(8,128)(2,1)S(1)}, u32[]{:S(2)}, u32[]{:S(2)}) collective-permute-start(bf16[64,768]{1,0:T(8,128)(2,1)S(1)} %fusion.3.refs_0_), channel_id=1, source_target_pairs={{0,16},{8,24},{16,0},{24,8},{1,17},{9,25},{17,1},{25,9},{2,18},{10... | collective-permute-start | bytes 294920 | tf_op jit(solution)/shard_map/ppermute | solution.py:252
  34.4 0.0 collective-permute-start.4
  34.4 3.8 %collective-permute-done.3.refs_1_ = bf16[64,768]{1,0:T(8,128)(2,1)S(1)} collective-permute-done((bf16[64,768]{1,0:T(8,128)(2,1)S(1)}, bf16[64,768]{1,0:T(8,128)(2,1)S(1)}, u32[]{:S(2)}, u32[]{:S(2)}) %collective-permute-start.3) | collective-permute-done | bytes 98336 | tf_op jit(solution)/shard_map/ppermute | solution.py:252
  38.2 0.0 collective-permute-start.5
  38.2 0.0 collective-permute-done.4.refs_2_
  38.2 1.3 %collective-permute-done.5.refs_3_ = bf16[64,768]{1,0:T(8,128)(2,1)S(1)} collective-permute-done((bf16[64,768]{1,0:T(8,128)(2,1)S(1)}, bf16[64,768]{1,0:T(8,128)(2,1)S(1)}, u32[]{:S(2)}, u32[]{:S(2)}) %collective-permute-start.5) | collective-permute-done | bytes 98336 | tf_op jit(solution)/shard_map/ppermute | solution.py:255
  39.5 0.0 copy-done.2
  39.5 20.1 %whiten.1 = (f32[192,768]{1,0:T(8,128)}, f32[768,512]{1,0:T(8,128)}) custom-call(s32[1]{0:T(128)} %bitcast.index_ref, bf16[768,512]{1,0:T(8,128)(2,1)S(1)} %bitcast.36, bf16[64,768]{1,0:T(8,128)(2,1)S(1)} %fusion.3.refs_0_, bf16[64,768]{1,0:T(8,128)(2,1)S(1)} %collective-permute-done.3.refs_1_, bf16[64,768]{1,0:T(8,128)(2,1)S(1)} %collective-permute-done.4.refs_2_, ...), custom_call_target="tpu_custom_call" | custom-call | tf_op jit(solution)/shard_map/whiten/pallas_call | solution.py:189
  (2 shorter events, 0.1 us)
Async XLA Ops:
  0.6 21.8 %copy-start = (bf16[1,512,768]{2,1,0:T(8,128)(2,1)S(1)}, bf16[1,512,768]{2,1,0:T(8,128)(2,1)}, u32[]{:S(2)}) copy-start(bf16[1,512,768]{2,1,0:T(8,128)(2,1)} %param.7) | copy-start | bytes 2359300
  0.6 21.8 %copy-start.1 = (bf16[1,512,768]{2,1,0:T(8,128)(2,1)S(1)}, bf16[1,512,768]{2,1,0:T(8,128)(2,1)}, u32[]{:S(2)}) copy-start(bf16[1,512,768]{2,1,0:T(8,128)(2,1)} %param.8) | copy-start | bytes 2359300
  0.7 21.7 %collective-permute-start = (bf16[512,768]{1,0:T(8,128)(2,1)}, bf16[512,768]{1,0:T(8,128)(2,1)S(1)}, u32[]{:S(2)}, u32[]{:S(2)}) collective-permute-start(bf16[512,768]{1,0:T(8,128)(2,1)} %bitcast.32), channel_id=1, source_target_pairs={{0,8},{8,0},{16,24},{24,16},{1,9},{9,1},{17,25},{25,17},{2,10},{10... | collective-permute-start | bytes 2359304 | tf_op jit(solution)/shard_map/ppermute | solution.py:255
  1.2 21.2 %collective-permute-start.1 = (bf16[512,768]{1,0:T(8,128)(2,1)}, bf16[512,768]{1,0:T(8,128)(2,1)S(1)}, u32[]{:S(2)}, u32[]{:S(2)}) collective-permute-start(bf16[512,768]{1,0:T(8,128)(2,1)} %bitcast.34), channel_id=1, source_target_pairs={{0,8},{8,0},{16,24},{24,16},{1,9},{9,1},{17,25},{25,17},{2,10},{10... | collective-permute-start | bytes 2359304 | tf_op jit(solution)/shard_map/ppermute | solution.py:255
  4.0 18.4 %all-to-all-start = ((bf16[16,8,1024]{2,1,0:T(8,128)(2,1)}), bf16[16,8,1024]{2,1,0:T(8,128)(2,1)S(1)}, u32[]{:S(2)}, u32[]{:S(2)}) async-start(bf16[16,8,1024]{2,1,0:T(8,128)(2,1)} %bitcast.37), calls=%async_computation | async-start | bytes 524288 | tf_op jit(solution)/shard_map/all_to_all | solution.py:276
  24.2 15.3 %copy-start.2 = (bf16[1,768,512]{2,1,0:T(8,128)(2,1)S(1)}, bf16[1,768,512]{2,1,0:T(8,128)(2,1)}, u32[]{:S(2)}) copy-start(bf16[1,768,512]{2,1,0:T(8,128)(2,1)} %param.9) | copy-start | bytes 2359300
  24.2 9.2 %collective-permute-start.2 = (f32[64,1536]{1,0:T(8,128)S(1)}, f32[64,1536]{1,0:T(8,128)S(1)}, u32[]{:S(2)}, u32[]{:S(2)}) collective-permute-start(f32[64,1536]{1,0:T(8,128)S(1)} %slice_bitcast_fusion), channel_id=1, source_target_pairs={{0,16},{8,24},{16,0},{24,8},{1,17},{9,25},{17,1},{25,9},{2,18},{10... | collective-permute-start | bytes 1179656 | tf_op jit(solution)/shard_map/ppermute | solution.py:252
  33.5 4.7 %collective-permute-start.3 = (bf16[64,768]{1,0:T(8,128)(2,1)S(1)}, bf16[64,768]{1,0:T(8,128)(2,1)S(1)}, u32[]{:S(2)}, u32[]{:S(2)}) collective-permute-start(bf16[64,768]{1,0:T(8,128)(2,1)S(1)} %fusion.3.refs_0_), channel_id=1, source_target_pairs={{0,16},{8,24},{16,0},{24,8},{1,17},{9,25},{17,1},{25,9},{2,18},{10... | collective-permute-start | bytes 294920 | tf_op jit(solution)/shard_map/ppermute | solution.py:252
  34.4 3.8 %collective-permute-start.4 = (bf16[64,768]{1,0:T(8,128)(2,1)S(1)}, bf16[64,768]{1,0:T(8,128)(2,1)S(1)}, u32[]{:S(2)}, u32[]{:S(2)}) collective-permute-start(bf16[64,768]{1,0:T(8,128)(2,1)S(1)} %fusion.3.refs_0_), channel_id=1, source_target_pairs={{0,8},{8,0},{16,24},{24,16},{1,9},{9,1},{17,25},{25,17},{2,10},{10... | collective-permute-start | bytes 294920 | tf_op jit(solution)/shard_map/ppermute | solution.py:255
  38.2 1.3 %collective-permute-start.5 = (bf16[64,768]{1,0:T(8,128)(2,1)S(1)}, bf16[64,768]{1,0:T(8,128)(2,1)S(1)}, u32[]{:S(2)}, u32[]{:S(2)}) collective-permute-start(bf16[64,768]{1,0:T(8,128)(2,1)S(1)} %collective-permute-done.3.refs_1_), channel_id=1, source_target_pairs={{0,8},{8,0},{16,24},{24,16},{1,9},{9,1},{17,25},{25,17},{2,10},{10... | collective-permute-start | bytes 294920 | tf_op jit(solution)/shard_map/ppermute | solution.py:255

commit v4 on v3

--- a/solution.py
+++ b/solution.py
@@ -17,6 +17,8 @@
 highest = lax.Precision.HIGHEST
 f32 = jnp.float32
 bf16 = jnp.bfloat16
+f16 = jnp.float16
+LINK_SCALE = 32.0
 
 
 def reciprocal(value):
@@ -86,7 +88,7 @@
         k = window * WINDOW
         first = window * per_window
         mine = range(first, first + per_window)
-        columns = [[jnp.broadcast_to(left[g][:, k + c : k + c + 1], (8, PANEL)) + zero for g in mine] for c in range(WINDOW)]
+        columns = [[jnp.broadcast_to(left[g][:, k + c : k + c + 1], (8, PANEL)) + zero if g == first else jnp.broadcast_to(left[g][:, k + c : k + c + 1], (8, PANEL)) for g in mine] for c in range(WINDOW)]
         (up_l, up_r), (w_l, w_r) = eliminate(columns, [[left[g] for g in mine], [right[g] for g in mine]])
         uppers += [jnp.where(lane8 >= row8 + 8 * g, u, 0.0) for g, u in zip(mine, up_l)]
         inverses += up_r
@@ -106,9 +108,8 @@
                 o = (i - near) * 8
                 left[i] = left[i] - chg_l[o : o + 8]
                 right[i] = right[i] - chg_r[o : o + 8]
-        if window == PANEL // WINDOW - 1:
-            result.append(jnp.concatenate(uppers, 0))
-            result.append(jnp.concatenate(inverses, 0))
+        if (k + WINDOW) % SUPER == 0:
+            result.append((jnp.concatenate(uppers[-SUPER // 8 :], 0), jnp.concatenate(inverses[-SUPER // 8 :], 0)))
         yield
 
 def whiten_kernel(scale, index_ref, down_ref, *refs):
@@ -158,20 +159,43 @@
     for b in range(1, blocks):
         work += [functools.partial(store_gram, b, lo, hi) for lo, hi in chunks(b * PANEL)]
         work.append(functools.partial(clear, b))
+    def first_half(p, upper, inverse):
+        s, e = p * PANEL, (p + 1) * PANEL
+        m = s + SUPER
+        u_ref[s:m, s:e] = upper
+        if e < width:
+            inverse_ref[p % 2, :SUPER] = inverse
+            a_next = a_ref[s:m, e : e + PANEL]
+            u_ref[s:m, e : e + PANEL] = jnp.dot(inverse[:, :SUPER], a_next, preferred_element_type=f32, precision=highest)
+
+    def first_gram(p):
+        s, e = p * PANEL, (p + 1) * PANEL
+        top = u_ref[s : s + SUPER, e : e + PANEL]
+        a_ref[e : e + PANEL, e : e + PANEL] = a_ref[e : e + PANEL, e : e + PANEL] - transposed_dot(top, top, highest)
+
+    half = SUPER // WINDOW
     for p in range(blocks):
         s, e = p * PANEL, (p + 1) * PANEL
+        m = s + SUPER
         result = []
         done = 0
         for i, _ in enumerate(factor_steps(block, result, zero)):
+            if i == half:
+                first_half(p, *result[0])
+            if i == half + 1 and e < width:
+                first_gram(p)
             upto = len(work) * (i + 1) // steps
             for job in work[done:upto]: job()
             done = upto
-        u_ref[s:e, s:e] = result[0]
+        upper, inverse = result[1]
+        u_ref[m:e, s:e] = upper
         if e < width:
-            inverse_ref[p % 2] = result[1]
-            nxt = jnp.dot(result[1], a_ref[s:e, e:e+PANEL], preferred_element_type=f32, precision=highest)
-            u_ref[s:e, e:e+PANEL] = nxt
-            block = a_ref[e:e+PANEL, e:e+PANEL] - transposed_dot(nxt, nxt, highest)
+            inverse_ref[p % 2, SUPER:] = inverse
+            low = jnp.dot(inverse, a_ref[s:e, e:e+PANEL], preferred_element_type=f32, precision=highest)
+            u_ref[m:e, e:e+PANEL] = low
+            block = jnp.concatenate([
+                a_ref[e + o : e + o + SUPER, e : e + PANEL] - transposed_dot(low[:, o : o + SUPER], low, highest)
+                for o in range(0, PANEL, SUPER)], 0)
             f = e + PANEL
             work = [functools.partial(panel, p, lo, hi) for lo, hi in chunks(f)]
             work += [functools.partial(trail, p, p + 1, lo, hi) for lo, hi in chunks(f)]
@@ -203,8 +227,9 @@
 
 
 def project_kernel(index_ref, token_ref, *refs):
-    *weight_refs, out_ref = refs
-    chips, slots, both = out_ref.shape
+    *weight_refs, send_ref, keep_ref = refs
+    slots, both = keep_ref.shape
+    chips = send_ref.shape[0] + 1
     width = both // 2
     depth = weight_refs[0].shape[0]
     chip, core = index_ref[0], index_ref[1]
@@ -221,17 +246,25 @@
                     preferred_element_type=f32,
                 )
                 total = part if total is None else total + part
-            out_ref[k, :, half * width : (half + 1) * width] = total
+            columns = slice(half * width, (half + 1) * width)
+            if k < chips - 1:
+                send_ref[k, :, columns] = total * LINK_SCALE
+            else:
+                keep_ref[:, columns] = total
 
 
 def project(index, tokens, weights, chips):
     vmem = pl.BlockSpec(memory_space=pltpu.VMEM)
     both = 2 * weights[0].shape[1]
+    slots = tokens.shape[0] // chips
     return pl.pallas_call(
         project_kernel,
-        out_shape=jax.ShapeDtypeStruct((chips, tokens.shape[0] // chips, both), f32),
+        out_shape=(
+            jax.ShapeDtypeStruct((chips - 1, slots, both), f32),
+            jax.ShapeDtypeStruct((slots, both), f32),
+        ),
         in_specs=[pl.BlockSpec(memory_space=pltpu.SMEM)] + [vmem] * (1 + len(weights)),
-        out_specs=vmem,
+        out_specs=(vmem, vmem),
         compiler_params=pltpu.CompilerParams(vmem_limit_bytes=48 * 2**20),
         name="project",
     )(index, tokens, *weights)
@@ -285,10 +318,9 @@
     slot_total = received.shape[0] // chips
 
     index = jnp.stack([chip, core]).astype(jnp.int32)
-    partial = project(index, received, weights, chips)
-    total = partial[chips - 1]
+    sent, total = project(index, received, weights, chips)
     for k in range(1, chips):
-        total = total + to_chip(partial[k - 1], k)
+        total = total + to_chip(sent[k - 1].astype(f16), k).astype(f32) * (1.0 / LINK_SCALE)
     gate_sum, up_sum = total[:, :width], total[:, width:]
     hidden = (gate_sum / (1.0 + jnp.exp(-gate_sum)) * up_sum).astype(bf16)
     rows = [hidden] + [to_chip(hidden, k) for k in range(1, chips)]

time: 59.8 us -> 56.6 us (0.946)
  waiting for transfers between devices: 23.1 us -> 19.2 us
  starting transfers between devices: 10.9 us -> 11.8 us
    ppermute x2, waiting for transfers between devices: 11.8 us -> 7.88 us  [to_chip(): return lax.ppermute(x, 'dp', steps)]
    ppermute x2, starting transfers between devices: 2.05 us -> 2.89 us  [to_chip(): return lax.ppermute(x, 'dp', steps)]
where the time goes in v4:
time: 56.6 us; the launch traced here: 56.3 us
  Pallas kernels  21.7 us (38%)
  waiting for transfers between devices  19.2 us (34%)
  starting transfers between devices  11.8 us (21%)
  matrix products  1.3 us (2%)
  other arithmetic  0.91 us (2%)
  local copies, waits for them, and re-layouts  0.74 us (1%)
  between operations  0.73 us (1%)
    pallas_call x1, Pallas kernels, whiten(): pl.pallas_call(functools.partial(whiten_kernel, 1.0 / slot_total), out_sh...  19.9 us
    all_to_all x1, waiting for transfers between devices, body(): lax.all_to_all(outgoing.reshape(chips * owners, CAP, model // chips), ('d...  10 us
    all_to_all x1, starting transfers between devices, body(): lax.all_to_all(outgoing.reshape(chips * owners, CAP, model // chips), ('d...  8.29 us
    ppermute x2, waiting for transfers between devices, to_chip(): return lax.ppermute(x, 'dp', steps)  7.88 us
    ppermute x2, starting transfers between devices, to_chip(): return lax.ppermute(x, 'dp', steps)  2.89 us
    pallas_call x1, Pallas kernels, project(): pl.pallas_call(project_kernel, out_shape=(jax.ShapeDtypeStruct((chips - 1...  1.75 us
    ppermute x4, waiting for transfers between devices, to_core(): return lax.ppermute(x, 'dp', [(i, i ^ 1) for i in range(dp_size)])  1.3 us
    dot_general x1, matrix products, body(): jnp.einsum('tec,tyd->yecd', placing, tokens.reshape(tok_rows, chips, mode...  1.17 us
  transfers between devices with their start and end apart: 7, of which 4 were waited for; matrix products, arithmetic and copies ran while one was open for 5% of the time, Pallas kernels for 0%

profile of v4, /device:TPU:0, one launch (start us, length us, event | category | flops | bytes accessed | tf_op | source)
XLA Modules:
  0.0 56.3 jit_solution(9105955559641069795)
XLA Ops:
  0.6 0.0 copy-start.1
  0.6 0.0 copy-start.2
  0.7 0.5 collective-permute-start
  1.2 0.1 collective-permute-start.1
  1.2 0.7 %fusion.3 = pred[64,8]{0,1:T(8,128)(4,1)S(1)} fusion(s32[64,8]{0,1:T(8,128)} %param.6), kind=kLoop, calls=%fused_computation.11 | loop fusion | flops 7680 | bytes 2560 | tf_op jit(solution)/shard_map/reduce_or | solution.py:294
  1.9 0.1 fusion.4
  2.1 1.2 %fusion = bf16[2,8,8,1024]{3,2,0,1:T(8,128)(2,1)S(1)} fusion(bf16[8,2,8,1024]{3,2,1,0:T(8,128)(2,1)} %bitcast.34, s32[64,8]{0,1:T(8,128)S(1)} %fusion.4, pred[64,8]{0,1:T(8,128)(4,1)S(1)} %fusion.3), kind=kOutput, calls=%fused_computation.1 | convolution fusion | flops 16916480 | bytes 526848 | tf_op jit(solution)/shard_map/tec,tyd->yecd/dot_general | solution.py:299
  3.3 0.7 %copy.13 = bf16[2,8,8,1024]{3,2,1,0:T(8,128)(2,1)} copy(bf16[2,8,8,1024]{3,2,0,1:T(8,128)(2,1)S(1)} %fusion) | data formatting | bytes 524288 | tf_op jit(solution)/shard_map/convert_element_type | solution.py:304
  4.0 8.3 %all-to-all-start = ((bf16[16,8,1024]{2,1,0:T(8,128)(2,1)}), bf16[16,8,1024]{2,1,0:T(8,128)(2,1)S(1)}, u32[]{:S(2)}, u32[]{:S(2)}) async-start(bf16[16,8,1024]{2,1,0:T(8,128)(2,1)} %bitcast.33), calls=%async_computation | async-start | bytes 524288 | tf_op jit(solution)/shard_map/all_to_all | solution.py:309
  12.3 0.1 pad_add_fusion.index_ref
  12.4 10.0 %all-to-all-done = bf16[16,8,1024]{2,1,0:T(8,128)(2,1)S(1)} async-done(((bf16[16,8,1024]{2,1,0:T(8,128)(2,1)}), bf16[16,8,1024]{2,1,0:T(8,128)(2,1)S(1)}, u32[]{:S(2)}, u32[]{:S(2)}) %all-to-all-start) | async-done | bytes 262176 | tf_op jit(solution)/shard_map/all_to_all | solution.py:309
  22.4 0.0 collective-permute-done.refs_2_
  22.4 0.0 collective-permute-done.1.refs_3_
  22.4 0.0 copy-done.1
  22.4 0.0 copy-done.2
  22.4 1.8 %project.1 = (f32[1,64,1536]{2,1,0:T(8,128)S(1)}, f32[64,1536]{1,0:T(8,128)S(1)}) custom-call(s32[2]{0:T(128)S(1)} %pad_add_fusion.index_ref, bf16[128,1024]{1,0:T(8,128)(2,1)S(1)} %bitcast.27, bf16[512,768]{1,0:T(8,128)(2,1)S(1)} %bitcast.30, bf16[512,768]{1,0:T(8,128)(2,1)S(1)} %bitcast.32, bf16[512,768]{1,0:T(8,128)(2,1)S(1)} %collective-permute-done.refs_2_, ...), custom_call_target="tpu_custom_call" | custom-call | tf_op jit(solution)/shard_map/project/pallas_call | solution.py:260
  24.2 0.0 copy-start
  24.2 1.2 %collective-permute-start.2 = (f16[64,1536]{1,0:T(8,128)(2,1)S(1)}, f16[64,1536]{1,0:T(8,128)(2,1)S(1)}, u32[]{:S(2)}, u32[]{:S(2)}) collective-permute-start(f16[64,1536]{1,0:T(8,128)(2,1)S(1)} %convert_bitcast_fusion), channel_id=1, source_target_pairs={{0,16},{8,24},{16,0},{24,8},{1,17},{9,25},{17,1},{25,9},{2,18},{10... | collective-permute-start | bytes 589832 | tf_op jit(solution)/shard_map/ppermute | solution.py:285
  25.4 4.9 %collective-permute-done.2 = f16[64,1536]{1,0:T(8,128)(2,1)S(1)} collective-permute-done((f16[64,1536]{1,0:T(8,128)(2,1)S(1)}, f16[64,1536]{1,0:T(8,128)(2,1)S(1)}, u32[]{:S(2)}, u32[]{:S(2)}) %collective-permute-start.2) | collective-permute-done | bytes 196640 | tf_op jit(solution)/shard_map/ppermute | solution.py:285
  30.4 0.1 fusion.2.refs_0_
  30.4 1.7 %collective-permute-start.3 = (bf16[64,768]{1,0:T(8,128)(2,1)S(1)}, bf16[64,768]{1,0:T(8,128)(2,1)S(1)}, u32[]{:S(2)}, u32[]{:S(2)}) collective-permute-start(bf16[64,768]{1,0:T(8,128)(2,1)S(1)} %fusion.2.refs_0_), channel_id=1, source_target_pairs={{0,16},{8,24},{16,0},{24,8},{1,17},{9,25},{17,1},{25,9},{2,18},{10... | collective-permute-start | bytes 294920 | tf_op jit(solution)/shard_map/ppermute | solution.py:285
  32.2 0.0 collective-permute-start.4
  32.2 2.9 %collective-permute-done.3.refs_1_ = bf16[64,768]{1,0:T(8,128)(2,1)S(1)} collective-permute-done((bf16[64,768]{1,0:T(8,128)(2,1)S(1)}, bf16[64,768]{1,0:T(8,128)(2,1)S(1)}, u32[]{:S(2)}, u32[]{:S(2)}) %collective-permute-start.3) | collective-permute-done | bytes 98336 | tf_op jit(solution)/shard_map/ppermute | solution.py:285
  35.1 0.0 collective-permute-start.5
  35.1 0.0 collective-permute-done.4.refs_2_
  35.1 1.3 %collective-permute-done.5.refs_3_ = bf16[64,768]{1,0:T(8,128)(2,1)S(1)} collective-permute-done((bf16[64,768]{1,0:T(8,128)(2,1)S(1)}, bf16[64,768]{1,0:T(8,128)(2,1)S(1)}, u32[]{:S(2)}, u32[]{:S(2)}) %collective-permute-start.5) | collective-permute-done | bytes 98336 | tf_op jit(solution)/shard_map/ppermute | solution.py:288
  36.4 0.0 copy-done
  36.4 19.9 %whiten.1 = (f32[192,768]{1,0:T(8,128)}, f32[768,512]{1,0:T(8,128)}) custom-call(s32[1]{0:T(128)} %bitcast.index_ref, bf16[768,512]{1,0:T(8,128)(2,1)S(1)} %bitcast.28, bf16[64,768]{1,0:T(8,128)(2,1)S(1)} %fusion.2.refs_0_, bf16[64,768]{1,0:T(8,128)(2,1)S(1)} %collective-permute-done.3.refs_1_, bf16[64,768]{1,0:T(8,128)(2,1)S(1)} %collective-permute-done.4.refs_2_, ...), custom_call_target="tpu_custom_call" | custom-call | tf_op jit(solution)/shard_map/whiten/pallas_call | solution.py:213
  (2 shorter events, 0.1 us)
Async XLA Ops:
  0.6 21.8 %copy-start.1 = (bf16[1,512,768]{2,1,0:T(8,128)(2,1)S(1)}, bf16[1,512,768]{2,1,0:T(8,128)(2,1)}, u32[]{:S(2)}) copy-start(bf16[1,512,768]{2,1,0:T(8,128)(2,1)} %param.7) | copy-start | bytes 2359300
  0.6 21.8 %copy-start.2 = (bf16[1,512,768]{2,1,0:T(8,128)(2,1)S(1)}, bf16[1,512,768]{2,1,0:T(8,128)(2,1)}, u32[]{:S(2)}) copy-start(bf16[1,512,768]{2,1,0:T(8,128)(2,1)} %param.8) | copy-start | bytes 2359300
  0.7 21.7 %collective-permute-start = (bf16[512,768]{1,0:T(8,128)(2,1)}, bf16[512,768]{1,0:T(8,128)(2,1)S(1)}, u32[]{:S(2)}, u32[]{:S(2)}) collective-permute-start(bf16[512,768]{1,0:T(8,128)(2,1)} %bitcast.29), channel_id=1, source_target_pairs={{0,8},{8,0},{16,24},{24,16},{1,9},{9,1},{17,25},{25,17},{2,10},{10... | collective-permute-start | bytes 2359304 | tf_op jit(solution)/shard_map/ppermute | solution.py:288
  1.2 21.2 %collective-permute-start.1 = (bf16[512,768]{1,0:T(8,128)(2,1)}, bf16[512,768]{1,0:T(8,128)(2,1)S(1)}, u32[]{:S(2)}, u32[]{:S(2)}) collective-permute-start(bf16[512,768]{1,0:T(8,128)(2,1)} %bitcast.31), channel_id=1, source_target_pairs={{0,8},{8,0},{16,24},{24,16},{1,9},{9,1},{17,25},{25,17},{2,10},{10... | collective-permute-start | bytes 2359304 | tf_op jit(solution)/shard_map/ppermute | solution.py:288
  4.0 18.4 %all-to-all-start = ((bf16[16,8,1024]{2,1,0:T(8,128)(2,1)}), bf16[16,8,1024]{2,1,0:T(8,128)(2,1)S(1)}, u32[]{:S(2)}, u32[]{:S(2)}) async-start(bf16[16,8,1024]{2,1,0:T(8,128)(2,1)} %bitcast.33), calls=%async_computation | async-start | bytes 524288 | tf_op jit(solution)/shard_map/all_to_all | solution.py:309
  24.2 12.3 %copy-start = (bf16[1,768,512]{2,1,0:T(8,128)(2,1)S(1)}, bf16[1,768,512]{2,1,0:T(8,128)(2,1)}, u32[]{:S(2)}) copy-start(bf16[1,768,512]{2,1,0:T(8,128)(2,1)} %param.9) | copy-start | bytes 2359300
  24.2 6.1 %collective-permute-start.2 = (f16[64,1536]{1,0:T(8,128)(2,1)S(1)}, f16[64,1536]{1,0:T(8,128)(2,1)S(1)}, u32[]{:S(2)}, u32[]{:S(2)}) collective-permute-start(f16[64,1536]{1,0:T(8,128)(2,1)S(1)} %convert_bitcast_fusion), channel_id=1, source_target_pairs={{0,16},{8,24},{16,0},{24,8},{1,17},{9,25},{17,1},{25,9},{2,18},{10... | collective-permute-start | bytes 589832 | tf_op jit(solution)/shard_map/ppermute | solution.py:285
  30.4 4.7 %collective-permute-start.3 = (bf16[64,768]{1,0:T(8,128)(2,1)S(1)}, bf16[64,768]{1,0:T(8,128)(2,1)S(1)}, u32[]{:S(2)}, u32[]{:S(2)}) collective-permute-start(bf16[64,768]{1,0:T(8,128)(2,1)S(1)} %fusion.2.refs_0_), channel_id=1, source_target_pairs={{0,16},{8,24},{16,0},{24,8},{1,17},{9,25},{17,1},{25,9},{2,18},{10... | collective-permute-start | bytes 294920 | tf_op jit(solution)/shard_map/ppermute | solution.py:285
  32.2 3.0 %collective-permute-start.4 = (bf16[64,768]{1,0:T(8,128)(2,1)S(1)}, bf16[64,768]{1,0:T(8,128)(2,1)S(1)}, u32[]{:S(2)}, u32[]{:S(2)}) collective-permute-start(bf16[64,768]{1,0:T(8,128)(2,1)S(1)} %fusion.2.refs_0_), channel_id=1, source_target_pairs={{0,8},{8,0},{16,24},{24,16},{1,9},{9,1},{17,25},{25,17},{2,10},{10... | collective-permute-start | bytes 294920 | tf_op jit(solution)/shard_map/ppermute | solution.py:288
  35.1 1.3 %collective-permute-start.5 = (bf16[64,768]{1,0:T(8,128)(2,1)S(1)}, bf16[64,768]{1,0:T(8,128)(2,1)S(1)}, u32[]{:S(2)}, u32[]{:S(2)}) collective-permute-start(bf16[64,768]{1,0:T(8,128)(2,1)S(1)} %collective-permute-done.3.refs_1_), channel_id=1, source_target_pairs={{0,8},{8,0},{16,24},{24,16},{1,9},{9,1},{17,25},{25,17},{2,10},{10... | collective-permute-start | bytes 294920 | tf_op jit(solution)/shard_map/ppermute | solution.py:288

commit v5 on v4

--- a/solution.py
+++ b/solution.py
@@ -113,13 +113,15 @@
         yield
 
 def whiten_kernel(scale, index_ref, down_ref, *refs):
-    *row_refs, factor_ref, out_ref, hidden_ref, a_ref, u_ref, inverse_ref = refs
+    *row_refs, factor_hbm, out_hbm, hidden_ref, a_ref, u_ref, inverse_ref, out_ref, sems = refs
     width = hidden_ref.shape[1]
     step = row_refs[0].shape[0]
     for i, row_ref in enumerate(row_refs):
         hidden_ref[i * step : (i + 1) * step, :] = row_ref[...]
     blocks = width // PANEL
     steps = PANEL // WINDOW
+    share = factor_hbm.shape[0]
+    leaving = []
     zero = jnp.full((8, PANEL), jnp.where(index_ref[0] < 0, 1.0, 0.0), f32)
 
     def gram(b, lo, hi):
@@ -150,6 +152,9 @@
         low = (rows - high.astype(f32)).astype(bf16)
         down = down_ref[s:, :]
         out_ref[s:e, :] = jnp.dot(high, down, preferred_element_type=f32) + jnp.dot(low, down, preferred_element_type=f32)
+        copy = pltpu.make_async_copy(out_ref.at[s:e], out_hbm.at[s:e], sems.at[p])
+        copy.start()
+        leaving.append(copy)
 
     def clear(p):
         if p: u_ref[p * PANEL : (p + 1) * PANEL, : p * PANEL] = jnp.zeros((PANEL, p * PANEL), f32)
@@ -202,10 +207,13 @@
             for b in range(p + 2, blocks):
                 work += [functools.partial(trail, p, b, lo, hi) for lo, hi in chunks(b * PANEL)]
             work.append(functools.partial(output, p))
-        else:
-            output(p)
-    share = factor_ref.shape[0]
-    factor_ref[...] = u_ref[pl.ds(pl.multiple_of(index_ref[0] * share, 8), share), :]
+    rows = pl.ds(pl.multiple_of(index_ref[0] * share, 8), share)
+    copy = pltpu.make_async_copy(u_ref.at[rows], factor_hbm, sems.at[blocks])
+    copy.start()
+    output(blocks - 1)
+    for item in leaving + [copy]:
+        item.wait()
+
 
 def whiten(index, rows, down, share, slot_total):
     width, columns = down.shape
@@ -214,12 +222,14 @@
         functools.partial(whiten_kernel, 1.0 / slot_total),
         out_shape=(jax.ShapeDtypeStruct((share, width), f32), jax.ShapeDtypeStruct((width, columns), f32)),
         in_specs=[pl.BlockSpec(memory_space=pltpu.SMEM), vmem] + [vmem] * len(rows),
-        out_specs=(vmem, vmem),
+        out_specs=(pl.BlockSpec(memory_space=pl.ANY), pl.BlockSpec(memory_space=pl.ANY)),
         scratch_shapes=[
             pltpu.VMEM((len(rows) * rows[0].shape[0], width), bf16),
             pltpu.VMEM((width, width), f32),
             pltpu.VMEM((width, width), f32),
             pltpu.VMEM((2, PANEL, PANEL), f32),
+            pltpu.VMEM((width, columns), f32),
+            pltpu.SemaphoreType.DMA((width // PANEL + 1,)),
         ],
         compiler_params=pltpu.CompilerParams(vmem_limit_bytes=48 * 2**20),
         name="whiten",

time: 56.6 us -> 56.4 us (level)
  no operation moved by 1% of the time
where the time goes in v5:
time: 56.4 us; the launch traced here: 56.1 us
  Pallas kernels  21.2 us (38%)
  waiting for transfers between devices  19.2 us (34%)
  starting transfers between devices  11.8 us (21%)
  matrix products  1.3 us (2%)
  other arithmetic  0.91 us (2%)
  between operations  0.89 us (2%)
  local copies, waits for them, and re-layouts  0.74 us (1%)
    pallas_call x1, Pallas kernels, whiten(): pl.pallas_call(functools.partial(whiten_kernel, 1.0 / slot_total), out_sh...  19.5 us
    all_to_all x1, waiting for transfers between devices, body(): lax.all_to_all(outgoing.reshape(chips * owners, CAP, model // chips), ('d...  10 us
    all_to_all x1, starting transfers between devices, body(): lax.all_to_all(outgoing.reshape(chips * owners, CAP, model // chips), ('d...  8.29 us
    ppermute x2, waiting for transfers between devices, to_chip(): return lax.ppermute(x, 'dp', steps)  7.88 us
    ppermute x2, starting transfers between devices, to_chip(): return lax.ppermute(x, 'dp', steps)  2.89 us
    pallas_call x1, Pallas kernels, project(): pl.pallas_call(project_kernel, out_shape=(jax.ShapeDtypeStruct((chips - 1...  1.75 us
    ppermute x4, waiting for transfers between devices, to_core(): return lax.ppermute(x, 'dp', [(i, i ^ 1) for i in range(dp_size)])  1.3 us
    dot_general x1, matrix products, body(): jnp.einsum('tec,tyd->yecd', placing, tokens.reshape(tok_rows, chips, mode...  1.17 us
  transfers between devices with their start and end apart: 7, of which 4 were waited for; matrix products, arithmetic and copies ran while one was open for 5% of the time, Pallas kernels for 0%

profile of v5, /device:TPU:0, one launch (start us, length us, event | category | flops | bytes accessed | tf_op | source)
XLA Modules:
  0.0 56.1 jit_solution(8255349516228962467)
XLA Ops:
  0.6 0.0 copy-start.1
  0.6 0.0 copy-start.2
  0.7 0.5 collective-permute-start
  1.2 0.1 collective-permute-start.1
  1.2 0.7 %fusion.3 = pred[64,8]{0,1:T(8,128)(4,1)S(1)} fusion(s32[64,8]{0,1:T(8,128)} %param.6), kind=kLoop, calls=%fused_computation.11 | loop fusion | flops 7680 | bytes 2560 | tf_op jit(solution)/shard_map/reduce_or | solution.py:304
  1.9 0.1 fusion.4
  2.1 1.2 %fusion = bf16[2,8,8,1024]{3,2,0,1:T(8,128)(2,1)S(1)} fusion(bf16[8,2,8,1024]{3,2,1,0:T(8,128)(2,1)} %bitcast.34, s32[64,8]{0,1:T(8,128)S(1)} %fusion.4, pred[64,8]{0,1:T(8,128)(4,1)S(1)} %fusion.3), kind=kOutput, calls=%fused_computation.1 | convolution fusion | flops 16916480 | bytes 526848 | tf_op jit(solution)/shard_map/tec,tyd->yecd/dot_general | solution.py:309
  3.3 0.7 %copy.13 = bf16[2,8,8,1024]{3,2,1,0:T(8,128)(2,1)} copy(bf16[2,8,8,1024]{3,2,0,1:T(8,128)(2,1)S(1)} %fusion) | data formatting | bytes 524288 | tf_op jit(solution)/shard_map/convert_element_type | solution.py:314
  4.0 8.3 %all-to-all-start = ((bf16[16,8,1024]{2,1,0:T(8,128)(2,1)}), bf16[16,8,1024]{2,1,0:T(8,128)(2,1)S(1)}, u32[]{:S(2)}, u32[]{:S(2)}) async-start(bf16[16,8,1024]{2,1,0:T(8,128)(2,1)} %bitcast.33), calls=%async_computation | async-start | bytes 524288 | tf_op jit(solution)/shard_map/all_to_all | solution.py:319
  12.3 0.1 pad_add_fusion.index_ref
  12.4 10.0 %all-to-all-done = bf16[16,8,1024]{2,1,0:T(8,128)(2,1)S(1)} async-done(((bf16[16,8,1024]{2,1,0:T(8,128)(2,1)}), bf16[16,8,1024]{2,1,0:T(8,128)(2,1)S(1)}, u32[]{:S(2)}, u32[]{:S(2)}) %all-to-all-start) | async-done | bytes 262176 | tf_op jit(solution)/shard_map/all_to_all | solution.py:319
  22.4 0.0 collective-permute-done.refs_2_
  22.4 0.0 collective-permute-done.1.refs_3_
  22.4 0.0 copy-done.1
  22.4 0.0 copy-done.2
  22.4 1.8 %project.1 = (f32[1,64,1536]{2,1,0:T(8,128)S(1)}, f32[64,1536]{1,0:T(8,128)S(1)}) custom-call(s32[2]{0:T(128)S(1)} %pad_add_fusion.index_ref, bf16[128,1024]{1,0:T(8,128)(2,1)S(1)} %bitcast.27, bf16[512,768]{1,0:T(8,128)(2,1)S(1)} %bitcast.30, bf16[512,768]{1,0:T(8,128)(2,1)S(1)} %bitcast.32, bf16[512,768]{1,0:T(8,128)(2,1)S(1)} %collective-permute-done.refs_2_, ...), custom_call_target="tpu_custom_call" | custom-call | tf_op jit(solution)/shard_map/project/pallas_call | solution.py:270
  24.2 0.0 copy-start
  24.2 1.2 %collective-permute-start.2 = (f16[64,1536]{1,0:T(8,128)(2,1)S(1)}, f16[64,1536]{1,0:T(8,128)(2,1)S(1)}, u32[]{:S(2)}, u32[]{:S(2)}) collective-permute-start(f16[64,1536]{1,0:T(8,128)(2,1)S(1)} %convert_bitcast_fusion), channel_id=1, source_target_pairs={{0,16},{8,24},{16,0},{24,8},{1,17},{9,25},{17,1},{25,9},{2,18},{10... | collective-permute-start | bytes 589832 | tf_op jit(solution)/shard_map/ppermute | solution.py:295
  25.4 4.9 %collective-permute-done.2 = f16[64,1536]{1,0:T(8,128)(2,1)S(1)} collective-permute-done((f16[64,1536]{1,0:T(8,128)(2,1)S(1)}, f16[64,1536]{1,0:T(8,128)(2,1)S(1)}, u32[]{:S(2)}, u32[]{:S(2)}) %collective-permute-start.2) | collective-permute-done | bytes 196640 | tf_op jit(solution)/shard_map/ppermute | solution.py:295
  30.4 0.1 fusion.2.refs_0_
  30.4 1.7 %collective-permute-start.3 = (bf16[64,768]{1,0:T(8,128)(2,1)S(1)}, bf16[64,768]{1,0:T(8,128)(2,1)S(1)}, u32[]{:S(2)}, u32[]{:S(2)}) collective-permute-start(bf16[64,768]{1,0:T(8,128)(2,1)S(1)} %fusion.2.refs_0_), channel_id=1, source_target_pairs={{0,16},{8,24},{16,0},{24,8},{1,17},{9,25},{17,1},{25,9},{2,18},{10... | collective-permute-start | bytes 294920 | tf_op jit(solution)/shard_map/ppermute | solution.py:295
  32.2 0.0 collective-permute-start.4
  32.2 2.9 %collective-permute-done.3.refs_1_ = bf16[64,768]{1,0:T(8,128)(2,1)S(1)} collective-permute-done((bf16[64,768]{1,0:T(8,128)(2,1)S(1)}, bf16[64,768]{1,0:T(8,128)(2,1)S(1)}, u32[]{:S(2)}, u32[]{:S(2)}) %collective-permute-start.3) | collective-permute-done | bytes 98336 | tf_op jit(solution)/shard_map/ppermute | solution.py:295
  35.1 0.0 collective-permute-start.5
  35.1 0.0 collective-permute-done.4.refs_2_
  35.1 1.3 %collective-permute-done.5.refs_3_ = bf16[64,768]{1,0:T(8,128)(2,1)S(1)} collective-permute-done((bf16[64,768]{1,0:T(8,128)(2,1)S(1)}, bf16[64,768]{1,0:T(8,128)(2,1)S(1)}, u32[]{:S(2)}, u32[]{:S(2)}) %collective-permute-start.5) | collective-permute-done | bytes 98336 | tf_op jit(solution)/shard_map/ppermute | solution.py:298
  36.4 0.0 copy-done
  36.4 19.5 %whiten.1 = (f32[192,768]{1,0:T(8,128)}, f32[768,512]{1,0:T(8,128)}) custom-call(s32[1]{0:T(128)} %bitcast.index_ref, bf16[768,512]{1,0:T(8,128)(2,1)S(1)} %bitcast.28, bf16[64,768]{1,0:T(8,128)(2,1)S(1)} %fusion.2.refs_0_, bf16[64,768]{1,0:T(8,128)(2,1)S(1)} %collective-permute-done.3.refs_1_, bf16[64,768]{1,0:T(8,128)(2,1)S(1)} %collective-permute-done.4.refs_2_, ...), custom_call_target="tpu_custom_call" | custom-call | tf_op jit(solution)/shard_map/whiten/pallas_call | solution.py:221
  (2 shorter events, 0.1 us)
Async XLA Ops:
  0.6 21.8 %copy-start.1 = (bf16[1,512,768]{2,1,0:T(8,128)(2,1)S(1)}, bf16[1,512,768]{2,1,0:T(8,128)(2,1)}, u32[]{:S(2)}) copy-start(bf16[1,512,768]{2,1,0:T(8,128)(2,1)} %param.7) | copy-start | bytes 2359300
  0.6 21.8 %copy-start.2 = (bf16[1,512,768]{2,1,0:T(8,128)(2,1)S(1)}, bf16[1,512,768]{2,1,0:T(8,128)(2,1)}, u32[]{:S(2)}) copy-start(bf16[1,512,768]{2,1,0:T(8,128)(2,1)} %param.8) | copy-start | bytes 2359300
  0.7 21.7 %collective-permute-start = (bf16[512,768]{1,0:T(8,128)(2,1)}, bf16[512,768]{1,0:T(8,128)(2,1)S(1)}, u32[]{:S(2)}, u32[]{:S(2)}) collective-permute-start(bf16[512,768]{1,0:T(8,128)(2,1)} %bitcast.29), channel_id=1, source_target_pairs={{0,8},{8,0},{16,24},{24,16},{1,9},{9,1},{17,25},{25,17},{2,10},{10... | collective-permute-start | bytes 2359304 | tf_op jit(solution)/shard_map/ppermute | solution.py:298
  1.2 21.2 %collective-permute-start.1 = (bf16[512,768]{1,0:T(8,128)(2,1)}, bf16[512,768]{1,0:T(8,128)(2,1)S(1)}, u32[]{:S(2)}, u32[]{:S(2)}) collective-permute-start(bf16[512,768]{1,0:T(8,128)(2,1)} %bitcast.31), channel_id=1, source_target_pairs={{0,8},{8,0},{16,24},{24,16},{1,9},{9,1},{17,25},{25,17},{2,10},{10... | collective-permute-start | bytes 2359304 | tf_op jit(solution)/shard_map/ppermute | solution.py:298
  4.0 18.4 %all-to-all-start = ((bf16[16,8,1024]{2,1,0:T(8,128)(2,1)}), bf16[16,8,1024]{2,1,0:T(8,128)(2,1)S(1)}, u32[]{:S(2)}, u32[]{:S(2)}) async-start(bf16[16,8,1024]{2,1,0:T(8,128)(2,1)} %bitcast.33), calls=%async_computation | async-start | bytes 524288 | tf_op jit(solution)/shard_map/all_to_all | solution.py:319
  24.2 12.3 %copy-start = (bf16[1,768,512]{2,1,0:T(8,128)(2,1)S(1)}, bf16[1,768,512]{2,1,0:T(8,128)(2,1)}, u32[]{:S(2)}) copy-start(bf16[1,768,512]{2,1,0:T(8,128)(2,1)} %param.9) | copy-start | bytes 2359300
  24.2 6.1 %collective-permute-start.2 = (f16[64,1536]{1,0:T(8,128)(2,1)S(1)}, f16[64,1536]{1,0:T(8,128)(2,1)S(1)}, u32[]{:S(2)}, u32[]{:S(2)}) collective-permute-start(f16[64,1536]{1,0:T(8,128)(2,1)S(1)} %convert_bitcast_fusion), channel_id=1, source_target_pairs={{0,16},{8,24},{16,0},{24,8},{1,17},{9,25},{17,1},{25,9},{2,18},{10... | collective-permute-start | bytes 589832 | tf_op jit(solution)/shard_map/ppermute | solution.py:295
  30.4 4.7 %collective-permute-start.3 = (bf16[64,768]{1,0:T(8,128)(2,1)S(1)}, bf16[64,768]{1,0:T(8,128)(2,1)S(1)}, u32[]{:S(2)}, u32[]{:S(2)}) collective-permute-start(bf16[64,768]{1,0:T(8,128)(2,1)S(1)} %fusion.2.refs_0_), channel_id=1, source_target_pairs={{0,16},{8,24},{16,0},{24,8},{1,17},{9,25},{17,1},{25,9},{2,18},{10... | collective-permute-start | bytes 294920 | tf_op jit(solution)/shard_map/ppermute | solution.py:295
  32.2 3.0 %collective-permute-start.4 = (bf16[64,768]{1,0:T(8,128)(2,1)S(1)}, bf16[64,768]{1,0:T(8,128)(2,1)S(1)}, u32[]{:S(2)}, u32[]{:S(2)}) collective-permute-start(bf16[64,768]{1,0:T(8,128)(2,1)S(1)} %fusion.2.refs_0_), channel_id=1, source_target_pairs={{0,8},{8,0},{16,24},{24,16},{1,9},{9,1},{17,25},{25,17},{2,10},{10... | collective-permute-start | bytes 294920 | tf_op jit(solution)/shard_map/ppermute | solution.py:298
  35.1 1.3 %collective-permute-start.5 = (bf16[64,768]{1,0:T(8,128)(2,1)S(1)}, bf16[64,768]{1,0:T(8,128)(2,1)S(1)}, u32[]{:S(2)}, u32[]{:S(2)}) collective-permute-start(bf16[64,768]{1,0:T(8,128)(2,1)S(1)} %collective-permute-done.3.refs_1_), channel_id=1, source_target_pairs={{0,8},{8,0},{16,24},{24,16},{1,9},{9,1},{17,25},{25,17},{2,10},{10... | collective-permute-start | bytes 294920 | tf_op jit(solution)/shard_map/ppermute | solution.py:298
